TPU v7x, 256 devices: a whole 4x4x8 slice. The times are simulated.
256 devices in a mesh: row: 16 (over z_hi, x, core), col: 16 (over y, z_lo).
Axes of the slice: x: 4, y: 4, z: 8 (z_hi: 2, z_lo: 4; z = z_hi * 4 + z_lo), core: 2. Of those that a mesh axis runs over, the one named last changes fastest.
Arguments:
- fine_state: bfloat16 [32, 128, 4096], P(None, 'row', 'col'), may hold values from -40 to 40
- coarse_state: bfloat16 [64, 64, 2048], P(None, 'row', 'col'), may hold values from -40 to 40
- fine_inject: bfloat16 [32, 128, 4096], P(None, 'row', 'col'), may hold values from -6 to 6
- coarse_inject: bfloat16 [64, 64, 2048], P(None, 'row', 'col'), may hold values from -6 to 6
- fine_cotangent: float32 [32, 128, 4096], P(None, 'row', 'col'), may hold values from -40 to 40
- coarse_cotangent: float32 [64, 64, 2048], P(None, 'row', 'col'), may hold values from -40 to 40
- fine_first: bfloat16 [9, 160, 32], replicated, may hold values from -0.375 to 0.375
- fine_second: bfloat16 [9, 32, 160], replicated, may hold values from -0.3125 to 0.3125
- coarse_first: bfloat16 [9, 320, 64], replicated, may hold values from -0.25 to 0.25
- coarse_second: bfloat16 [9, 64, 320], replicated, may hold values from -0.25 to 0.25
- fine_gain: float32 [160], replicated, may hold values from 0.1 to 1.9
- fine_shift: float32 [160], replicated, may hold values from -3 to 3
- coarse_gain: float32 [320], replicated, may hold values from 0.1 to 1.9
- coarse_shift: float32 [320], replicated, may hold values from -3 to 3
- reduction_weight: bfloat16 [2, 2, 64, 32], replicated, may hold values from -0.5 to 0.5
- weight_up: bfloat16 [32, 64], replicated, may hold values from -0.75 to 0.75
Outputs:
- adjoint_fine: float32 [32, 128, 4096], P(None, 'row', 'col')
- adjoint_coarse: float32 [64, 64, 2048], P(None, 'row', 'col')
All inputs are finite; a program needn't handle non-finite values.
Results may differ from a plain program's by a relative error of at most 0.02.
Values may be sent and summed in bfloat16 or wider, within the bound.
A program may use at most 128 MiB of HBM per device.

v0:
```python
import jax
import jax.numpy as jnp
from jax import lax
from jax.sharding import PartitionSpec as P

GROUPS = 4
ITERS = 3


EPSILON = 1e-05


def extended(shard, sides, width):
    for axis, dim in sides:
        peers, length = (lax.axis_size(axis), shard.shape[dim])
        up = [(i, (i + 1) % peers) for i in range(peers - 1)]
        down = [(j, i) for i, j in up]
        last = lax.slice_in_dim(shard, length - width, length, axis=dim)
        leading = lax.slice_in_dim(shard, 0, width, axis=dim)
        before = lax.ppermute(last, axis, up)
        after = lax.ppermute(leading, axis, down)
        shard = jnp.concatenate([before, shard, after], axis=dim)
    return shard


def swish_derivative(value):
    sigma = jax.nn.sigmoid(value)
    return sigma * (1.0 + value * (1.0 - sigma))


def conv_valid(padded, weights):
    height = padded.shape[1] - 2
    width = padded.shape[2] - 2
    total = jnp.zeros((weights.shape[1], height, width), jnp.float32)
    for tap in range(9):
        row_shift = tap // 3
        col_shift = tap % 3
        window = padded[:, row_shift : row_shift + height, col_shift : col_shift + width]
        total = total + jnp.einsum(
            "oc,chw->ohw", weights[tap], window, preferred_element_type=jnp.float32
        )
    return total


def conv_back(padded, weights):
    height = padded.shape[1] - 2
    width = padded.shape[2] - 2
    total = jnp.zeros((weights.shape[2], height, width), jnp.float32)
    for tap in range(9):
        row_shift = tap // 3
        col_shift = tap % 3
        window = padded[
            :, 2 - row_shift : 2 - row_shift + height, 2 - col_shift : 2 - col_shift + width
        ]
        total = total + jnp.einsum(
            "oc,ohw->chw", weights[tap], window, preferred_element_type=jnp.float32
        )
    return total


def reduce_resolution(fine_tensor, reduction_weight):
    channels, rows, cols = fine_tensor.shape
    blocks = fine_tensor.reshape(channels, rows // 2, 2, cols // 2, 2)
    return jnp.einsum(
        "aboc,chawb->ohw", reduction_weight, blocks, preferred_element_type=jnp.float32
    )


def reduce_resolution_reverse(coarse_tensor, reduction_weight):
    spread = jnp.einsum(
        "aboc,ohw->chawb", reduction_weight, coarse_tensor, preferred_element_type=jnp.float32
    )
    return spread.reshape(spread.shape[0], spread.shape[1] * 2, spread.shape[3] * 2)


def upsample(coarse_tensor, weight_up):
    projected = jnp.einsum(
        "co,ohw->chw", weight_up, coarse_tensor, preferred_element_type=jnp.float32
    )
    channels, rows, cols = projected.shape
    wide = jnp.broadcast_to(projected[:, :, None, :, None], (channels, rows, 2, cols, 2))
    return wide.reshape(channels, rows * 2, cols * 2)


def upsample_back(fine_tensor, weight_up):
    channels, rows, cols = fine_tensor.shape
    blocks = fine_tensor.reshape(channels, rows // 2, 2, cols // 2, 2)
    return jnp.einsum("co,chawb->ohw", weight_up, blocks, preferred_element_type=jnp.float32)


def per_channel(values, channels):
    return jnp.repeat(values, channels // values.shape[0])[:, None, None]


def group_sums(field):
    return jnp.sum(field.reshape(GROUPS, -1), axis=1)


def inner(first, second):
    return jnp.sum(first[0] * second[0]) + jnp.sum(first[1] * second[1])


def combine(first, second, factor):
    return (first[0] + factor * second[0], first[1] + factor * second[1])


def extend(field):
    return extended(field, (("row", 1), ("col", 2)), 1)


def extend_pair(fine_tensor, coarse_tensor):
    return (extend(fine_tensor), extend(coarse_tensor))


def body(
    fine_state,
    coarse_state,
    fine_inject,
    coarse_inject,
    fine_cotangent,
    coarse_cotangent,
    fine_first,
    fine_second,
    coarse_first,
    coarse_second,
    fine_gain,
    fine_shift,
    coarse_gain,
    coarse_shift,
    reduction_weight,
    weight_up,
):
    injects = (fine_inject, coarse_inject)
    firsts = (fine_first, coarse_first)
    seconds = (fine_second, coarse_second)
    gains = (fine_gain, coarse_gain)
    shifts = (fine_shift, coarse_shift)
    shapes = (fine_state.shape, coarse_state.shape)
    widened = (fine_first.shape[1], coarse_first.shape[1])
    devices = lax.axis_size("row") * lax.axis_size("col")
    counts = tuple(
        (
            widened[stream] // GROUPS * shapes[stream][1] * shapes[stream][2] * devices
            for stream in range(2)
        )
    )
    grown_states = extend_pair(fine_state, coarse_state)
    pres = tuple((conv_valid(grown_states[stream], firsts[stream]) for stream in range(2)))
    inside_pres = tuple((pres[stream] for stream in range(2)))
    fine_local = jnp.stack(
        [group_sums(inside_pres[0]), group_sums(inside_pres[0] * inside_pres[0])]
    )
    coarse_local = jnp.stack(
        [group_sums(inside_pres[1]), group_sums(inside_pres[1] * inside_pres[1])]
    )
    stats = lax.psum((fine_local, coarse_local), ("row", "col"))
    normeds = []
    inverses = []
    level_slopes = []
    activations = []
    for stream in range(2):
        channels = widened[stream]
        mean = stats[stream][0] / counts[stream]
        variance = stats[stream][1] / counts[stream] - mean * mean
        inverse = lax.rsqrt(variance + EPSILON)
        normed = (pres[stream] - per_channel(mean, channels)) * per_channel(inverse, channels)
        level = normed * gains[stream][:, None, None] + shifts[stream][:, None, None]
        activations.append(jax.nn.silu(level))
        normeds.append(normed)
        inverses.append(inverse)
        level_slopes.append(swish_derivative(level))
    hidden_ins = extend_pair(
        activations[0].astype(jnp.bfloat16), activations[1].astype(jnp.bfloat16)
    )
    blended_list = [
        conv_valid(hidden_ins[stream], seconds[stream]) + injects[stream].astype(jnp.float32)
        for stream in range(2)
    ]
    fine_slope = swish_derivative(
        blended_list[0] + upsample(blended_list[1].astype(jnp.bfloat16), weight_up)
    )
    coarse_derivative = swish_derivative(
        blended_list[1] + reduce_resolution(blended_list[0].astype(jnp.bfloat16), reduction_weight)
    )
    cotangent = (fine_cotangent, coarse_cotangent)
    solution = (jnp.zeros_like(fine_cotangent), jnp.zeros_like(coarse_cotangent))
    previous = cotangent
    update = cotangent
    lefts = []
    rights = []
    for step in range(ITERS):
        moved = update
        solution = combine(solution, moved, 1.0)
        fine_gradient = solution[0] * fine_slope
        coarse_gradient = solution[1] * coarse_derivative
        grown_totals = extend_pair(
            (
                fine_gradient
                + reduce_resolution_reverse(coarse_gradient.astype(jnp.bfloat16), reduction_weight)
            ).astype(jnp.bfloat16),
            (coarse_gradient + upsample_back(fine_gradient.astype(jnp.bfloat16), weight_up)).astype(
                jnp.bfloat16
            ),
        )
        scaled_all = []
        local_grads = []
        for adjoint_stream in range(2):
            hidden_grad = conv_back(grown_totals[adjoint_stream], seconds[adjoint_stream])
            scaled = (
                hidden_grad * level_slopes[adjoint_stream] * gains[adjoint_stream][:, None, None]
            )
            inside_normed = normeds[adjoint_stream]
            local_grads.append(jnp.stack([group_sums(scaled), group_sums(scaled * inside_normed)]))
            scaled_all.append(scaled)
        grad_sums = lax.psum((local_grads[0], local_grads[1]), ("row", "col"))
        pre_grads = []
        for adjoint_stream in range(2):
            adjoint_channels = widened[adjoint_stream]
            first_mean = per_channel(
                grad_sums[adjoint_stream][0] / counts[adjoint_stream], adjoint_channels
            )
            second_mean = per_channel(
                grad_sums[adjoint_stream][1] / counts[adjoint_stream], adjoint_channels
            )
            pre_grads.append(
                per_channel(inverses[adjoint_stream], adjoint_channels)
                * (scaled_all[adjoint_stream] - first_mean - normeds[adjoint_stream] * second_mean)
            )
        pre_ins = extend_pair(pre_grads[0].astype(jnp.bfloat16), pre_grads[1].astype(jnp.bfloat16))
        image = (conv_back(pre_ins[0], firsts[0]), conv_back(pre_ins[1], firsts[1]))
        now = combine(combine(image, cotangent, 1.0), solution, -1.0)
        if step + 1 < ITERS:
            change = combine(now, previous, -1.0)
            terms = len(lefts)
            local = (
                [inner(right, change) for right in rights]
                + [inner(moved, left) for left in lefts]
                + [inner(right, now) for right in rights]
                + [inner(moved, moved)]
            )
            totals = lax.psum(jnp.stack(local), ("row", "col"))
            along_change = totals[0:terms]
            along_left = totals[terms : 2 * terms]
            along_now = totals[2 * terms : 3 * terms]
            moved_square = totals[3 * terms]
            back = (-change[0], -change[1])
            row_term = (-moved[0], -moved[1])
            for term in range(terms):
                back = combine(back, lefts[term], along_change[term])
                row_term = combine(row_term, rights[term], along_left[term])
            pair = lax.psum(
                jnp.stack([inner(row_term, change), inner(row_term, now)]), ("row", "col")
            )
            curvature_value = pair[0]
            new_weight = pair[1]
            denominator = jnp.maximum(curvature_value, 0.25 * moved_square)
            difference = combine(moved, back, -1.0)
            new_left = (difference[0] / denominator, difference[1] / denominator)
            update = now
            for term in range(terms):
                update = combine(update, lefts[term], -along_now[term])
            update = combine(update, new_left, -new_weight)
            lefts.append(new_left)
            rights.append(row_term)
            previous = now
    return (solution[0], solution[1])


def solution(mesh):
    placed = (
        P(None, "row", "col"),
        P(None, "row", "col"),
        P(None, "row", "col"),
        P(None, "row", "col"),
        P(None, "row", "col"),
        P(None, "row", "col"),
        P(),
        P(),
        P(),
        P(),
        P(),
        P(),
        P(),
        P(),
        P(),
        P(),
    )
    return jax.shard_map(
        body,
        mesh=mesh,
        in_specs=placed,
        out_specs=(P(None, "row", "col"), P(None, "row", "col")),
        check_vma=False,
    )
```

profile of v0, /device:TPU:1, one launch (start us, length us, event | category | flops | bytes accessed | tf_op | source)
XLA Modules:
  0.0 878.7 jit_solution(11239922137026736536)
XLA Ops:
  1.7 4.5 collective-permute-start
  18.7 4.2 collective-permute-start.2
  25.0 4.2 collective-permute-start.10
  38.9 95.1 %all-reduce.3 = (f32[2,4]{1,0:T(2,128)S(1)}, f32[2,4]{1,0:T(2,128)S(1)}) all-reduce(f32[2,4]{1,0:T(2,128)S(1)} %pad_maximum_fusion.53, f32[2,4]{1,0:T(2,128)S(1)} %copy-done.55), channel_id=1, replica_groups=mesh['row'=16,'col'=16] {'row','col'}, use_global_device_ids=true, to_apply=%region_9.10 | all-reduce | flops 16 | bytes 128 | tf_op jit(solution)/shard_map/psum | solution.py:156
  154.2 4.8 collective-permute-start.14
  164.6 8.7 collective-permute-done.7
  177.4 16.2 %collective-permute-done.15 = bf16[320,6,1]{2,0,1:T(8,128)(2,1)} collective-permute-done((bf16[320,6,1]{2,0,1:T(8,128)(2,1)}, bf16[320,6,1]{2,0,1:T(8,128)(2,1)}, u32[]{:S(2)}, u32[]{:S(2)}) %collective-permute-start.15) | collective-permute-done | bytes 3872 | tf_op jit(solution)/shard_map/ppermute | solution.py:21
  208.5 3.9 collective-permute-start.16
  220.2 3.6 collective-permute-start.24
  225.3 4.0 collective-permute-start.19
  230.7 4.8 collective-permute-start.27
  251.1 93.2 %all-reduce.2 = (f32[2,4]{1,0:T(2,128)S(1)}, f32[2,4]{1,0:T(2,128)}) all-reduce(f32[2,4]{1,0:T(2,128)S(1)} %pad_maximum_fusion.55, f32[2,4]{1,0:T(2,128)S(1)} %pad_maximum_fusion.54), channel_id=1, replica_groups=mesh['row'=16,'col'=16] {'row','col'}, use_global_device_ids=true, to_apply=%region_21.22 | all-reduce | flops 16 | bytes 128 | tf_op jit(solution)/shard_map/psum | solution.py:215
  366.7 4.0 collective-permute-start.31
  372.4 4.2 collective-permute-start.23
  377.5 21.4 %collective-permute-done.22 = bf16[160,10,1]{2,0,1:T(8,128)(2,1)S(1)} collective-permute-done((bf16[160,10,1]{2,0,1:T(8,128)(2,1)S(1)}, bf16[160,10,1]{2,0,1:T(8,128)(2,1)S(1)}, u32[]{:S(2)}, u32[]{:S(2)}) %collective-permute-start.22) | collective-permute-done | bytes 3232 | tf_op jit(solution)/shard_map/ppermute | solution.py:21
  408.3 90.9 %all-reduce.1 = (f32[2]{0:T(128)S(1)}, f32[1]{0:T(128)}) all-reduce(f32[2]{0:T(128)S(1)} %pad_maximum_fusion.58, f32[1]{0:T(128)} %bitcast.121), channel_id=1, replica_groups=mesh['row'=16,'col'=16] {'row','col'}, use_global_device_ids=true, to_apply=%region_25.26 | all-reduce | flops 3 | bytes 24 | tf_op jit(solution)/shard_map/psum | solution.py:251
  526.3 4.6 collective-permute-start.43
  532.4 4.2 collective-permute-start.35
  550.3 89.9 %all-reduce = (f32[2,4]{1,0:T(2,128)}, f32[2,4]{1,0:T(2,128)S(1)}) all-reduce(f32[2,4]{1,0:T(2,128)S(1)} %pad_maximum_fusion.56, f32[2,4]{1,0:T(2,128)S(1)} %pad_maximum_fusion.57), channel_id=1, replica_groups=mesh['row'=16,'col'=16] {'row','col'}, use_global_device_ids=true, to_apply=%region_33.34 | all-reduce | flops 16 | bytes 128 | tf_op jit(solution)/shard_map/psum | solution.py:215
  659.2 4.3 collective-permute-start.47
  665.2 4.3 collective-permute-start.39
  670.4 21.4 %collective-permute-done.38 = bf16[160,10,1]{2,0,1:T(8,128)(2,1)S(1)} collective-permute-done((bf16[160,10,1]{2,0,1:T(8,128)(2,1)S(1)}, bf16[160,10,1]{2,0,1:T(8,128)(2,1)S(1)}, u32[]{:S(2)}, u32[]{:S(2)}) %collective-permute-start.38) | collective-permute-done | bytes 3232 | tf_op jit(solution)/shard_map/ppermute | solution.py:21
  703.4 89.5 %psum.78 = f32[4]{0:T(128)S(1)} all-reduce(f32[4]{0:T(128)S(1)} %pad_maximum_fusion.59), channel_id=1, replica_groups=mesh['row'=16,'col'=16] {'row','col'}, use_global_device_ids=true, to_apply=%region_48.49 | all-reduce | flops 4 | bytes 32 | tf_op jit(solution)/shard_map/psum | solution.py:241
  798.8 73.0 %psum.79 = f32[2]{0:T(128)S(1)} all-reduce(f32[2]{0:T(128)S(1)} %pad_maximum_fusion.60), channel_id=1, replica_groups=mesh['row'=16,'col'=16] {'row','col'}, use_global_device_ids=true, to_apply=%region_53.54 | all-reduce | flops 2 | bytes 16 | tf_op jit(solution)/shard_map/psum | solution.py:251
  (479 shorter events, 200.9 us)
Async XLA Ops:
  1.7 14.6 %collective-permute-start = (bf16[32,1,256]{2,0,1:T(8,128)(2,1)S(1)}, bf16[32,1,256]{2,0,1:T(8,128)(2,1)S(1)}, u32[]{:S(2)}, u32[]{:S(2)}) collective-permute-start(bf16[32,1,256]{2,0,1:T(8,128)(2,1)S(1)} %get-tuple-element.101), channel_id=1, source_target_pairs={{0,16},{16,32},{32,48},{48,64},{64,80},{80,96},{96,112},{112,128},... | collective-permute-start | bytes 49160 | tf_op jit(solution)/shard_map/ppermute | solution.py:20
  9.0 13.9 %collective-permute-start.8 = (bf16[64,1,128]{2,0,1:T(8,128)(2,1)S(1)}, bf16[64,1,128]{2,0,1:T(8,128)(2,1)S(1)}, u32[]{:S(2)}, u32[]{:S(2)}) collective-permute-start(bf16[64,1,128]{2,0,1:T(8,128)(2,1)S(1)} %get-tuple-element.117), channel_id=1, source_target_pairs={{0,16},{16,32},{32,48},{48,64},{64,80},{80,96},{96,112},{112,128},... | collective-permute-start | bytes 49160 | tf_op jit(solution)/shard_map/ppermute | solution.py:20
  135.9 13.9 %collective-permute-start.4 = (bf16[160,1,256]{2,0,1:T(8,128)(2,1)}, bf16[160,1,256]{2,0,1:T(8,128)(2,1)S(1)}, u32[]{:S(2)}, u32[]{:S(2)}) collective-permute-start(bf16[160,1,256]{2,0,1:T(8,128)(2,1)} %get-tuple-element.66), channel_id=1, source_target_pairs={{0,16},{16,32},{32,48},{48,64},{64,80},{80,96},{96,112},{112,128},... | collective-permute-start | bytes 245768 | tf_op jit(solution)/shard_map/ppermute | solution.py:20
  150.1 14.5 %collective-permute-start.6 = (bf16[160,10,1]{2,0,1:T(8,128)(2,1)S(1)}, bf16[160,10,1]{2,0,1:T(8,128)(2,1)S(1)}, u32[]{:S(2)}, u32[]{:S(2)}) collective-permute-start(bf16[160,10,1]{2,0,1:T(8,128)(2,1)S(1)} %get-tuple-element.58), channel_id=1, source_target_pairs={{0,1},{1,2},{2,3},{3,4},{4,5},{5,6},{6,7},{7,8},{8,9},{9,10},{10,1... | collective-permute-start | bytes 9608 | tf_op jit(solution)/shard_map/ppermute | solution.py:20
  151.7 21.6 %collective-permute-start.7 = (bf16[160,10,1]{2,0,1:T(8,128)(2,1)S(1)}, bf16[160,10,1]{2,0,1:T(8,128)(2,1)S(1)}, u32[]{:S(2)}, u32[]{:S(2)}) collective-permute-start(bf16[160,10,1]{2,0,1:T(8,128)(2,1)S(1)} %get-tuple-element.59), channel_id=1, source_target_pairs={{1,0},{2,1},{3,2},{4,3},{5,4},{6,5},{7,6},{8,7},{9,8},{10,9},{11,1... | collective-permute-start | bytes 9608 | tf_op jit(solution)/shard_map/ppermute | solution.py:21
  154.2 23.1 %collective-permute-start.14 = (bf16[320,6,1]{2,0,1:T(8,128)(2,1)}, bf16[320,6,1]{2,0,1:T(8,128)(2,1)}, u32[]{:S(2)}, u32[]{:S(2)}) collective-permute-start(bf16[320,6,1]{2,0,1:T(8,128)(2,1)} %get-tuple-element.78), channel_id=1, source_target_pairs={{0,1},{1,2},{2,3},{3,4},{4,5},{5,6},{6,7},{7,8},{8,9},{9,10},{10,1... | collective-permute-start | bytes 11528 | tf_op jit(solution)/shard_map/ppermute | solution.py:20
  159.0 34.5 %collective-permute-start.15 = (bf16[320,6,1]{2,0,1:T(8,128)(2,1)}, bf16[320,6,1]{2,0,1:T(8,128)(2,1)}, u32[]{:S(2)}, u32[]{:S(2)}) collective-permute-start(bf16[320,6,1]{2,0,1:T(8,128)(2,1)} %get-tuple-element.79), channel_id=1, source_target_pairs={{1,0},{2,1},{3,2},{4,3},{5,4},{6,5},{7,6},{8,7},{9,8},{10,9},{11,1... | collective-permute-start | bytes 11528 | tf_op jit(solution)/shard_map/ppermute | solution.py:21
  206.5 17.3 %collective-permute-start.17 = (bf16[32,1,256]{2,0,1:T(8,128)(2,1)S(1)}, bf16[32,1,256]{2,0,1:T(8,128)(2,1)S(1)}, u32[]{:S(2)}, u32[]{:S(2)}) collective-permute-start(bf16[32,1,256]{2,0,1:T(8,128)(2,1)S(1)} %get-tuple-element.99), channel_id=1, source_target_pairs={{16,0},{32,16},{48,32},{64,48},{80,64},{96,80},{112,96},{128,112},... | collective-permute-start | bytes 49160 | tf_op jit(solution)/shard_map/ppermute | solution.py:21
  208.5 15.3 %collective-permute-start.16 = (bf16[32,1,256]{2,0,1:T(8,128)(2,1)S(1)}, bf16[32,1,256]{2,0,1:T(8,128)(2,1)S(1)}, u32[]{:S(2)}, u32[]{:S(2)}) collective-permute-start(bf16[32,1,256]{2,0,1:T(8,128)(2,1)S(1)} %get-tuple-element.98), channel_id=1, source_target_pairs={{0,16},{16,32},{32,48},{48,64},{64,80},{80,96},{96,112},{112,128},... | collective-permute-start | bytes 49160 | tf_op jit(solution)/shard_map/ppermute | solution.py:20
  224.0 14.6 %collective-permute-start.18 = (bf16[32,10,1]{2,0,1:T(8,128)(2,1)S(1)}, bf16[32,10,1]{2,0,1:T(8,128)(2,1)S(1)}, u32[]{:S(2)}, u32[]{:S(2)}) collective-permute-start(bf16[32,10,1]{2,0,1:T(8,128)(2,1)S(1)} %get-tuple-element.92), channel_id=1, source_target_pairs={{1,0},{2,1},{3,2},{4,3},{5,4},{6,5},{7,6},{8,7},{9,8},{10,9},{11,1... | collective-permute-start | bytes 1928 | tf_op jit(solution)/shard_map/ppermute | solution.py:21
  229.4 14.6 %collective-permute-start.26 = (bf16[64,6,1]{2,0,1:T(8,128)(2,1)S(1)}, bf16[64,6,1]{2,0,1:T(8,128)(2,1)}, u32[]{:S(2)}, u32[]{:S(2)}) collective-permute-start(bf16[64,6,1]{2,0,1:T(8,128)(2,1)S(1)} %get-tuple-element.108), channel_id=1, source_target_pairs={{1,0},{2,1},{3,2},{4,3},{5,4},{6,5},{7,6},{8,7},{9,8},{10,9},{11,1... | collective-permute-start | bytes 2312 | tf_op jit(solution)/shard_map/ppermute | solution.py:21
  346.8 18.4 %collective-permute-start.29 = (bf16[320,1,128]{2,0,1:T(8,128)(2,1)}, bf16[320,1,128]{2,0,1:T(8,128)(2,1)S(1)}, u32[]{:S(2)}, u32[]{:S(2)}) collective-permute-start(bf16[320,1,128]{2,0,1:T(8,128)(2,1)} %get-tuple-element.83), channel_id=1, source_target_pairs={{16,0},{32,16},{48,32},{64,48},{80,64},{96,80},{112,96},{128,112},... | collective-permute-start | bytes 245768 | tf_op jit(solution)/shard_map/ppermute | solution.py:21
  349.4 15.8 %collective-permute-start.28 = (bf16[320,1,128]{2,0,1:T(8,128)(2,1)S(1)}, bf16[320,1,128]{2,0,1:T(8,128)(2,1)S(1)}, u32[]{:S(2)}, u32[]{:S(2)}) collective-permute-start(bf16[320,1,128]{2,0,1:T(8,128)(2,1)S(1)} %get-tuple-element.82), channel_id=1, source_target_pairs={{0,16},{16,32},{32,48},{48,64},{64,80},{80,96},{96,112},{112,128},... | collective-permute-start | bytes 245768 | tf_op jit(solution)/shard_map/ppermute | solution.py:20
  365.4 37.5 %collective-permute-start.30 = (bf16[320,6,1]{2,0,1:T(8,128)(2,1)S(1)}, bf16[320,6,1]{2,0,1:T(8,128)(2,1)S(1)}, u32[]{:S(2)}, u32[]{:S(2)}) collective-permute-start(bf16[320,6,1]{2,0,1:T(8,128)(2,1)S(1)} %get-tuple-element.74), channel_id=1, source_target_pairs={{1,0},{2,1},{3,2},{4,3},{5,4},{6,5},{7,6},{8,7},{9,8},{10,9},{11,1... | collective-permute-start | bytes 11528 | tf_op jit(solution)/shard_map/ppermute | solution.py:21
  366.7 36.2 %collective-permute-start.31 = (bf16[320,6,1]{2,0,1:T(8,128)(2,1)S(1)}, bf16[320,6,1]{2,0,1:T(8,128)(2,1)S(1)}, u32[]{:S(2)}, u32[]{:S(2)}) collective-permute-start(bf16[320,6,1]{2,0,1:T(8,128)(2,1)S(1)} %get-tuple-element.75), channel_id=1, source_target_pairs={{0,1},{1,2},{2,3},{3,4},{4,5},{5,6},{6,7},{7,8},{8,9},{9,10},{10,1... | collective-permute-start | bytes 11528 | tf_op jit(solution)/shard_map/ppermute | solution.py:20
  371.1 27.8 %collective-permute-start.22 = (bf16[160,10,1]{2,0,1:T(8,128)(2,1)S(1)}, bf16[160,10,1]{2,0,1:T(8,128)(2,1)S(1)}, u32[]{:S(2)}, u32[]{:S(2)}) collective-permute-start(bf16[160,10,1]{2,0,1:T(8,128)(2,1)S(1)} %get-tuple-element.54), channel_id=1, source_target_pairs={{1,0},{2,1},{3,2},{4,3},{5,4},{6,5},{7,6},{8,7},{9,8},{10,9},{11,1... | collective-permute-start | bytes 9608 | tf_op jit(solution)/shard_map/ppermute | solution.py:21
  372.4 26.5 %collective-permute-start.23 = (bf16[160,10,1]{2,0,1:T(8,128)(2,1)S(1)}, bf16[160,10,1]{2,0,1:T(8,128)(2,1)S(1)}, u32[]{:S(2)}, u32[]{:S(2)}) collective-permute-start(bf16[160,10,1]{2,0,1:T(8,128)(2,1)S(1)} %get-tuple-element.55), channel_id=1, source_target_pairs={{0,1},{1,2},{2,3},{3,4},{4,5},{5,6},{6,7},{7,8},{8,9},{9,10},{10,1... | collective-permute-start | bytes 9608 | tf_op jit(solution)/shard_map/ppermute | solution.py:20
  525.0 19.7 %collective-permute-start.42 = (bf16[64,6,1]{2,0,1:T(8,128)(2,1)}, bf16[64,6,1]{2,0,1:T(8,128)(2,1)S(1)}, u32[]{:S(2)}, u32[]{:S(2)}) collective-permute-start(bf16[64,6,1]{2,0,1:T(8,128)(2,1)} %get-tuple-element.104), channel_id=1, source_target_pairs={{1,0},{2,1},{3,2},{4,3},{5,4},{6,5},{7,6},{8,7},{9,8},{10,9},{11,1... | collective-permute-start | bytes 2312 | tf_op jit(solution)/shard_map/ppermute | solution.py:21
  526.3 18.4 %collective-permute-start.43 = (bf16[64,6,1]{2,0,1:T(8,128)(2,1)}, bf16[64,6,1]{2,0,1:T(8,128)(2,1)}, u32[]{:S(2)}, u32[]{:S(2)}) collective-permute-start(bf16[64,6,1]{2,0,1:T(8,128)(2,1)} %get-tuple-element.105), channel_id=1, source_target_pairs={{0,1},{1,2},{2,3},{3,4},{4,5},{5,6},{6,7},{7,8},{8,9},{9,10},{10,1... | collective-permute-start | bytes 2312 | tf_op jit(solution)/shard_map/ppermute | solution.py:20
  643.4 14.2 %collective-permute-start.45 = (bf16[320,1,128]{2,0,1:T(8,128)(2,1)}, bf16[320,1,128]{2,0,1:T(8,128)(2,1)S(1)}, u32[]{:S(2)}, u32[]{:S(2)}) collective-permute-start(bf16[320,1,128]{2,0,1:T(8,128)(2,1)} %get-tuple-element.81), channel_id=1, source_target_pairs={{16,0},{32,16},{48,32},{64,48},{80,64},{96,80},{112,96},{128,112},... | collective-permute-start | bytes 245768 | tf_op jit(solution)/shard_map/ppermute | solution.py:21
  657.9 37.5 %collective-permute-start.46 = (bf16[320,6,1]{2,0,1:T(8,128)(2,1)S(1)}, bf16[320,6,1]{2,0,1:T(8,128)(2,1)S(1)}, u32[]{:S(2)}, u32[]{:S(2)}) collective-permute-start(bf16[320,6,1]{2,0,1:T(8,128)(2,1)S(1)} %get-tuple-element.70), channel_id=1, source_target_pairs={{1,0},{2,1},{3,2},{4,3},{5,4},{6,5},{7,6},{8,7},{9,8},{10,9},{11,1... | collective-permute-start | bytes 11528 | tf_op jit(solution)/shard_map/ppermute | solution.py:21
  659.2 36.2 %collective-permute-start.47 = (bf16[320,6,1]{2,0,1:T(8,128)(2,1)S(1)}, bf16[320,6,1]{2,0,1:T(8,128)(2,1)S(1)}, u32[]{:S(2)}, u32[]{:S(2)}) collective-permute-start(bf16[320,6,1]{2,0,1:T(8,128)(2,1)S(1)} %get-tuple-element.71), channel_id=1, source_target_pairs={{0,1},{1,2},{2,3},{3,4},{4,5},{5,6},{6,7},{7,8},{8,9},{9,10},{10,1... | collective-permute-start | bytes 11528 | tf_op jit(solution)/shard_map/ppermute | solution.py:20
  663.9 27.9 %collective-permute-start.38 = (bf16[160,10,1]{2,0,1:T(8,128)(2,1)S(1)}, bf16[160,10,1]{2,0,1:T(8,128)(2,1)S(1)}, u32[]{:S(2)}, u32[]{:S(2)}) collective-permute-start(bf16[160,10,1]{2,0,1:T(8,128)(2,1)S(1)} %get-tuple-element.50), channel_id=1, source_target_pairs={{1,0},{2,1},{3,2},{4,3},{5,4},{6,5},{7,6},{8,7},{9,8},{10,9},{11,1... | collective-permute-start | bytes 9608 | tf_op jit(solution)/shard_map/ppermute | solution.py:21
  665.2 26.6 %collective-permute-start.39 = (bf16[160,10,1]{2,0,1:T(8,128)(2,1)S(1)}, bf16[160,10,1]{2,0,1:T(8,128)(2,1)S(1)}, u32[]{:S(2)}, u32[]{:S(2)}) collective-permute-start(bf16[160,10,1]{2,0,1:T(8,128)(2,1)S(1)} %get-tuple-element.51), channel_id=1, source_target_pairs={{0,1},{1,2},{2,3},{3,4},{4,5},{5,6},{6,7},{7,8},{8,9},{9,10},{10,1... | collective-permute-start | bytes 9608 | tf_op jit(solution)/shard_map/ppermute | solution.py:20
  (94 other events, 1386.2 us)
where the time goes:
time: 889 us; the launch traced here: 879 us
  blocking collectives  532 us (60%)
  starting transfers between devices  133 us (15%)
  waiting for transfers between devices  67.8 us (8%)
  matrix products  59.1 us (7%)
  local copies, waits for them, and re-layouts  35.7 us (4%)
  other arithmetic  33 us (4%)
  between operations  18.8 us (2%)
    psum x2, blocking collectives, body(): grad_sums = lax.psum((local_grads[0], local_grads[1]), ('row', 'col'))  183 us
    psum x2, blocking collectives, body(): lax.psum(jnp.stack([inner(row_term, change), inner(row_term, now)]), ('ro...  164 us
    psum x1, blocking collectives, body(): stats = lax.psum((fine_local, coarse_local), ('row', 'col'))  95.1 us
    ppermute x24, starting transfers between devices, extended(): before = lax.ppermute(last, axis, up)  91.6 us
    psum x1, blocking collectives, body(): totals = lax.psum(jnp.stack(local), ('row', 'col'))  89.5 us
    ppermute x24, waiting for transfers between devices, extended(): after = lax.ppermute(leading, axis, down)  67.8 us
    ppermute x24, starting transfers between devices, extended(): after = lax.ppermute(leading, axis, down)  41.1 us
    dot_general x72, matrix products, conv_back(): jnp.einsum('oc,ohw->chw', weights[tap], window, preferred_element_type=jn...  38.2 us
  transfers between devices with their start and end apart: 48, of which 4 were waited for; matrix products, arithmetic and copies ran while one was open for 7% of the time, Pallas kernels for 0%

commit v1 on v0

v1 whole, which is shorter than its diff:
```python
import functools

import jax
import jax.numpy as jnp
from jax import lax
from jax.experimental import pallas as pl
from jax.experimental.pallas import tpu as pltpu
from jax.sharding import PartitionSpec as P

GROUPS = 4
EPSILON = 1e-05
MESH = pl.DeviceIdType.MESH
F32 = jnp.float32
BF16 = jnp.bfloat16
DIRS = [(dr, dc) for dr in (-1, 0, 1) for dc in (-1, 0, 1) if dr or dc]
STATE, COT, TOTAL0, TOTAL1, IMAGE = range(5)


class Stream:
    def __init__(self, n, w, rows, cols):
        self.n, self.w, self.R, self.W = n, w, rows, cols
        self.gs = w // GROUPS
        self.main = (rows + 2) * cols
        self.NL = self.main + 128
        self.cells = rows * cols
        self.own = slice(2 * cols, 2 * cols + rows * cols)


def dot(a, b):
    return jnp.dot(a, b, preferred_element_type=F32)


def lanes_of(shape):
    return lax.broadcasted_iota(jnp.int32, shape, len(shape) - 1)


def subs_of(shape):
    return lax.broadcasted_iota(jnp.int32, shape, 0)


def roll(x, shift):
    return pltpu.roll(x, shift % x.shape[1], 1)


def wide_lanes(x, width):
    return x if width == 128 else jnp.concatenate([x] * (width // 128), axis=1)


def fold(x):
    return jnp.sum(x.reshape(x.shape[0] // 8, 8, x.shape[1]), axis=0)


def block(i, size):
    return pl.ds(pl.multiple_of(i * size, 128), size)


def swish_derivative(v):
    sigma = jax.nn.sigmoid(v)
    return sigma * (1.0 + v * (1.0 - sigma))


def to_row(accs):
    row = jnp.zeros((1, 128), F32)
    sub, lane = subs_of((8, 128)), lanes_of((8, 128))
    for first in range(0, len(accs), 8):
        stack = jnp.zeros((8, 128), F32)
        for k, acc in enumerate(accs[first : first + 8]):
            stack = jnp.where(sub == k, jnp.sum(acc, axis=0, keepdims=True), stack)
        col = jnp.sum(stack, axis=1, keepdims=True)
        row = row + jnp.sum(jnp.where(lane == sub + first, col, 0.0), axis=0, keepdims=True)
    return row


def pick(row, k):
    return jnp.sum(jnp.where(lanes_of((1, 128)) == k, row, 0.0), axis=1, keepdims=True)


def put_rows(s, rows, xm, pk):
    lane = lanes_of((s.n, 128))
    packed = jnp.zeros((s.n, 128), F32)
    for r, x in enumerate(rows):
        xm[:, (r + 2) * s.W : (r + 3) * s.W] = x.astype(BF16)
        x = x.astype(F32)
        edge = jnp.where(lane < 2, x[:, :128], jnp.where(lane >= 126, x[:, s.W - 128 :], 0.0))
        packed = packed + roll(edge, 8 * (r + 2) + 2)
    pk[...] = jnp.where(lane % 8 <= 2, packed, roll(packed, 2)).astype(BF16)


def edge_of(s, pk, pr):
    lane = lanes_of((s.n, 128))
    q = lane % 8

    def across(left, mid, right):
        return jnp.where(q <= 1, left, jnp.where(q <= 3, mid, right))

    own = (lane >= 16) & (lane < 16 + 8 * s.R)
    if pr is None:
        return jnp.where(own & (q >= 2) & (q <= 3), pk[...].astype(F32), 0.0)
    got = {d: pr[k].astype(F32) for k, d in enumerate(DIRS)}
    mid = across(got[0, -1], pk[...].astype(F32), got[0, 1])
    top = across(got[-1, -1], got[-1, 0], got[-1, 1])
    bottom = across(got[1, -1], got[1, 0], got[1, 1])
    return jnp.where(own, mid, jnp.where(lane < 16, roll(top, -8 * s.R), roll(bottom, 8 * s.R)))


def build(s, xm, edge, x3, x9, ring):
    n, W = s.n, s.W
    lane = lanes_of((n, 128))
    joined = jnp.where(lane % 8 == 0, roll(edge, -4), edge)
    lane = lanes_of((n, W))
    for k in range(s.R + 4):
        at = slice(k * W, (k + 1) * W)
        if not ring and not 2 <= k < s.R + 2:
            x3[:, at] = jnp.zeros((3 * n, W), BF16)
            continue
        x = xm[:, at]
        xf = x.astype(F32)
        t = wide_lanes(roll(joined, -(8 * k + 1)), W)
        x3[0:n, at] = jnp.where(lane == 0, t, roll(xf, 1)).astype(BF16)
        x3[n : 2 * n, at] = x
        x3[2 * n : 3 * n, at] = jnp.where(lane == W - 1, t, roll(xf, -1)).astype(BF16)
    for i in range(3):
        for j in range(3):
            x9[i, j * n : (j + 1) * n, :] = roll(edge, -(8 * i + j)).astype(BF16)


def widen(s, weights, x3, x9, out, inside=False):
    skip = s.W if inside else 0

    def step(b, _):
        total = dot(weights[0], x3[:, pl.ds(pl.multiple_of(b * 256 + skip, 128), 256)])
        for i in (1, 2):
            total = total + dot(weights[i], x3[:, pl.ds(pl.multiple_of(b * 256 + skip + i * s.W, 128), 256)])
        out[:, block(b, 256)] = total
        return 0

    lax.fori_loop(0, (s.cells if inside else s.main) // 256, step, 0)
    if not inside:
        out[:, s.main :] = dot(weights[0], x9[0]) + dot(weights[1], x9[1]) + dot(weights[2], x9[2])


def narrow(s, weights, h, z):
    n, W = s.n, s.W

    def step(b, _):
        total = dot(weights[0], h[:, block(b, 256)])
        for i in (1, 2):
            total = total + dot(weights[i], h[:, pl.ds(pl.multiple_of(b * 256 + i * W, 128), 256)])
        z[:, block(b, 256)] = total
        return 0

    lax.fori_loop(0, s.cells // 256, step, 0)
    edges = [dot(weights[i], h[:, s.main :]) for i in range(3)]
    total = edges[0] + roll(edges[1], -8) + roll(edges[2], -16)
    q = lanes_of((n, 128)) % 8
    joined = jnp.where(q == 1, roll(total[:n], 1), roll(total[2 * n :], -3))
    lane = lanes_of((n, W))

    def row(r):
        at = slice(r * W, (r + 1) * W)
        t = wide_lanes(roll(joined, -(8 * r + 1)), W)
        left = jnp.where(lane == 0, t, roll(z[0:n, at], 1))
        right = jnp.where(lane == W - 1, t, roll(z[2 * n : 3 * n, at], -1))
        return left + z[n : 2 * n, at] + right

    return row


def kernel(streams, sizes, *refs):
    f, c = streams
    (
        fine_state, coarse_state, fine_inject, coarse_inject, fine_cot, coarse_cot,
        fine_first, fine_second, coarse_first, coarse_second,
        fine_gain, fine_shift, coarse_gain, coarse_shift, reduction, up,
        fine_out, coarse_out,
        *rest,
    ) = refs
    (xm_f, xm_c, pk_f, pk_c, pr_f, pr_c, x3_f, x3_c, x9_f, x9_c,
     nm_f, nm_c, ls_f, ls_c, hg_f, hg_c, hb_f, hb_c, kc_f, kc_c, kp_f, kp_c,
     z_f, z_c, sl_f, sl_c, e_f, e_c, mk_f, mk_c, ga_f, ga_c, sh_f, sh_c,
     a1_f, a1_c, a3_f, a3_c, a4_f, a4_c, dup, split, rt, rw, u4, stack_f, stack_c, taps,
     ar_a, ar_b, halo_send, halo_recv, ar_send, ar_recv) = rest
    xm, pk, pr, x3, x9 = (xm_f, xm_c), (pk_f, pk_c), (pr_f, pr_c), (x3_f, x3_c), (x9_f, x9_c)
    nm, ls, hg, hb = (nm_f, nm_c), (ls_f, ls_c), (hg_f, hg_c), (hb_f, hb_c)
    kc, kp, zs, sl, es, mk = (kc_f, kc_c), (kp_f, kp_c), (z_f, z_c), (sl_f, sl_c), (e_f, e_c), (mk_f, mk_c)
    ga, sh, a1, a3, a4 = (ga_f, ga_c), (sh_f, sh_c), (a1_f, a1_c), (a3_f, a3_c), (a4_f, a4_c)
    first, second = (fine_first, coarse_first), (fine_second, coarse_second)
    cot, state = (fine_cot, coarse_cot), (fine_state, coarse_state)
    inject, outs = (fine_inject, coarse_inject), (fine_out, coarse_out)
    rows, cols, low_rows, low_cols = sizes
    high_rows, high_cols = rows // low_rows, cols // low_cols
    row, col = lax.axis_index("row"), lax.axis_index("col")
    both = (0, 1)

    def has(d):
        return (row + d[0] >= 0) & (row + d[0] < rows) & (col + d[1] >= 0) & (col + d[1] < cols)

    size_a, size_b = low_rows * high_cols, high_rows * low_cols
    me_a = (row % low_rows) * high_cols + col // low_cols
    me_b = (row // low_rows) * low_cols + col % low_cols

    def peer_a(k):
        p = (me_a + k) % size_a
        return ((row // low_rows) * low_rows + p // high_cols, (p % high_cols) * low_cols + col % low_cols)

    def peer_b(k):
        p = (me_b + k) % size_b
        return ((p // low_cols) * low_rows + row % low_rows, (col // low_cols) * low_cols + p % low_cols)

    def exchange_copies(s, k):
        W, R = streams[s].W, streams[s].R
        field = 2 * k + s
        made = []
        for i, d in enumerate(DIRS):
            back = DIRS.index((-d[0], -d[1]))
            made.append((pltpu.make_async_remote_copy(
                src_ref=pk[s].at[k], dst_ref=pr[s].at[k, back],
                send_sem=halo_send.at[field, i], recv_sem=halo_recv.at[field, back],
                device_id=(row + d[0], col + d[1]), device_id_type=MESH), d))
        for i, d, src, dst in ((8, (-1, 0), 2 * W, (R + 2) * W), (9, (1, 0), R * W, 0)):
            made.append((pltpu.make_async_remote_copy(
                src_ref=xm[s].at[k, :, pl.ds(src, 2 * W)], dst_ref=xm[s].at[k, :, pl.ds(dst, 2 * W)],
                send_sem=halo_send.at[field, i], recv_sem=halo_recv.at[field, i],
                device_id=(row + d[0], col), device_id_type=MESH), d))
        return made

    def exchange_start(s, k):
        for copy, d in exchange_copies(s, k):
            pl.when(has(d))(copy.start)

    def exchange_wait(s, k):
        W, R = streams[s].W, streams[s].R
        field = 2 * k + s
        for i, d in enumerate(DIRS):
            pl.when(has(d))(pltpu.make_async_copy(pk[s].at[k], pr[s].at[k, i], halo_recv.at[field, i]).wait)
        for i, d, dst in ((8, (1, 0), (R + 2) * W), (9, (-1, 0), 0)):
            ref = xm[s].at[k, :, pl.ds(dst, 2 * W)]
            pl.when(has(d))(pltpu.make_async_copy(ref, ref, halo_recv.at[field, i]).wait)

    def exchange_end(s, k):
        for copy, d in exchange_copies(s, k):
            pl.when(has(d))(copy.wait_send)

    def spread(k, stage, buf, me, size, peer):
        def send(p, _):
            pltpu.make_async_remote_copy(
                src_ref=buf.at[k, me], dst_ref=buf.at[k, me],
                send_sem=ar_send.at[k, stage], recv_sem=ar_recv.at[k, stage],
                device_id=peer(p), device_id_type=MESH).start()
            return 0

        lax.fori_loop(1, size, send, 0)

    def collect(k, stage, buf, size):
        ref = buf.at[k, pl.ds(0, size - 1)]
        pltpu.make_async_copy(ref, ref, ar_recv.at[k, stage]).wait()
        return jnp.sum(buf[k], axis=0)

    def reduce_start(k, value):
        ar_a[k, me_a] = value
        spread(k, 0, ar_a, me_a, size_a, peer_a)

    def reduce_middle(k):
        ar_b[k, me_b] = collect(k, 0, ar_a, size_a)
        spread(k, 1, ar_b, me_b, size_b, peer_b)

    def reduce_end(k):
        return collect(k, 1, ar_b, size_b)

    def reduce_drain(k):
        for stage, buf, size in ((0, ar_a, size_a), (1, ar_b, size_b)):
            ref = buf.at[k, pl.ds(0, size - 1)]
            pltpu.make_async_copy(ref, ref, ar_send.at[k, stage]).wait()

    for s in both:
        W, R = streams[s].W, streams[s].R
        for k in range(5):
            pr[s][k] = jnp.zeros(pr[s].shape[1:], BF16)
            xm[s][k, :, 0 : 2 * W] = jnp.zeros((streams[s].n, 2 * W), BF16)
            xm[s][k, :, (R + 2) * W : (R + 4) * W] = jnp.zeros((streams[s].n, 2 * W), BF16)
    barrier = pltpu.get_barrier_semaphore()

    def greet(device):
        pl.semaphore_signal(barrier, inc=1, device_id=device, device_id_type=MESH)

    for d in DIRS:
        pl.when(has(d))(functools.partial(greet, (row + d[0], col + d[1])))

    def greet_a(k, _):
        greet(peer_a(k))
        return 0

    def greet_b(k, _):
        greet(peer_b(k))
        return 0

    lax.fori_loop(1, size_a, greet_a, 0)
    lax.fori_loop(1, size_b, greet_b, 0)
    for s in both:
        put_rows(streams[s], [state[s][:, r, :].astype(F32) for r in range(streams[s].R)], xm[s].at[STATE], pk[s].at[STATE])
    beside = sum(has(d).astype(jnp.int32) for d in DIRS)
    pl.semaphore_wait(barrier, beside + (size_a + size_b - 2))
    for s in both:
        exchange_start(s, STATE)
    for s in both:
        put_rows(streams[s], [cot[s][:, r, :] for r in range(streams[s].R)], xm[s].at[COT], pk[s].at[COT])
    for s in both:
        exchange_start(s, COT)

    for s in both:
        n, w, W = streams[s].n, streams[s].w, streams[s].W
        for i in range(3):
            flipped = []
            for j in range(3):
                tap = first[s][3 * i + j].T
                taps[j * n : (j + 1) * n, 0:w] = tap
                a4[s][2 - i, (2 - j) * n : (3 - j) * n, :] = tap
            a1[s][i] = taps[0 : 3 * n, 0:w].T
            for j in range(3):
                t = 8 - (3 * i + j)
                taps[j * n : (j + 1) * n, 0:w] = second[s][t // 3, (t % 3) * n : (t % 3 + 1) * n, :]
            a3[s][i] = taps[0 : 3 * n, 0:w].T
        same = subs_of((w, w)) == lanes_of((w, w))
        for src, dst in (((fine_gain, coarse_gain)[s], ga[s]), ((fine_shift, coarse_shift)[s], sh[s])):
            dst[...] = jnp.broadcast_to(jnp.sum(jnp.where(same, src[...], 0.0), axis=1, keepdims=True), (w, 128))
        R = streams[s].R
        mk[s][...] = jnp.ones((1, streams[s].NL), F32)
        mk[s][:, 0:W] = jnp.where(row > 0, 1.0, 0.0) * jnp.ones((1, W), F32)
        mk[s][:, (R + 1) * W : (R + 2) * W] = jnp.where(row < rows - 1, 1.0, 0.0) * jnp.ones((1, W), F32)
        lane = lanes_of((1, 128))
        q, line = lane % 8, lane // 8
        good = ((q == 0) & (col > 0)) | ((q == 3) & (col < cols - 1))
        good = good & (line < R + 2) & ((line > 0) | (row > 0)) & ((line < R + 1) | (row < rows - 1))
        mk[s][:, streams[s].main :] = jnp.where(good, 1.0, 0.0)
    here, there = subs_of((128, 256)), lanes_of((128, 256))
    dup[...] = jnp.where(there // 2 == here, 1.0, 0.0).astype(BF16)
    here, there = subs_of((256, 256)), lanes_of((256, 256))
    split[...] = jnp.where(here == 2 * (there % 128) + there // 128, 1.0, 0.0).astype(BF16)
    for a in range(2):
        for b in range(2):
            at = slice((2 * a + b) * f.n, (2 * a + b + 1) * f.n)
            rt[at, :] = reduction[a, b].T
            taps[at, 0 : c.n] = up[...]
    rw[...] = rt[...].T
    u4[...] = taps[0 : 4 * f.n, 0 : c.n].T

    def load(s, k, ring=True):
        st = streams[s]
        edge = edge_of(st, pk[s].at[k], pr[s].at[k] if ring else None)
        build(st, xm[s].at[k], edge, x3[s], x9[s], ring)

    def group_loop(s, start, chunks, count, body):
        gs = streams[s].gs
        sums = []
        for g in range(GROUPS):
            at = slice(g * gs, (g + 1) * gs)

            def step(k, accs):
                return tuple(a + fold(t) for a, t in zip(accs, body(g, at, k + start)))

            sums.append(lax.fori_loop(0, chunks, step, (jnp.zeros((8, 128), F32),) * count))
        return [[sums[g][t] for g in range(GROUPS)] for t in range(count)]

    def ring_chunks(s):
        return 0, streams[s].NL // 128

    def own_chunks(s):
        return streams[s].W // 128, streams[s].cells // 128

    def flat(per_stream, t):
        return [a for s in both for a in per_stream[s][t]]

    sums = []
    for s in both:
        exchange_wait(s, STATE)
        load(s, STATE)
        widen(streams[s], a1[s], x3[s], x9[s], nm[s])

        def squares(g, at, k):
            x = nm[s][at, block(k, 128)]
            return x, x * x

        sums.append(group_loop(s, *own_chunks(s), 2, squares))
    reduce_start(0, to_row(flat(sums, 0) + flat(sums, 1)))
    for s in both:
        exchange_wait(s, COT)
        load(s, COT)
        widen(streams[s], a1[s], x3[s], x9[s], kc[s], inside=True)
    reduce_middle(0)
    stats = reduce_end(0)

    lane = lanes_of((1, 128))
    counts = [rows * cols * streams[s].cells * streams[s].gs for s in both]
    per = jnp.where(lane % 8 < GROUPS, 1.0 / counts[0], 1.0 / counts[1])
    mean_row = stats * per
    variance = roll(mean_row, -8) - mean_row * mean_row
    inverse_row = jnp.where(lane < 8, lax.rsqrt(variance + EPSILON), 0.0)
    means = [[pick(mean_row, s * GROUPS + g) for g in range(GROUPS)] for s in both]
    inverses = [[pick(inverse_row, s * GROUPS + g) for g in range(GROUPS)] for s in both]

    for s in both:
        gs = streams[s].gs
        for g in range(GROUPS):
            at = slice(g * gs, (g + 1) * gs)

            def activate(k, _):
                here = block(k, 128)
                gain, keep = ga[s][at, :], mk[s][:, here]
                normed = (nm[s][at, here] - means[s][g]) * inverses[s][g]
                level = normed * gain + sh[s][at, :]
                sigma = jax.nn.sigmoid(level)
                nm[s][at, here] = normed
                hb[s][at, here] = (level * sigma * keep).astype(BF16)
                ls[s][at, here] = sigma * (1.0 + level * (1.0 - sigma)) * gain * keep
                return 0

            lax.fori_loop(0, streams[s].NL // 128, activate, 0)

    def own_row(s, ref, r):
        return ref[:, r * streams[s].W : (r + 1) * streams[s].W]

    def halve():
        parts = dot(stack_f[...], split[...]).astype(BF16)
        lined = []
        for R in range(c.R):
            lined.append(jnp.concatenate([
                parts[(2 * R + a) * f.n : (2 * R + a + 1) * f.n, b * 128 : (b + 1) * 128]
                for a in range(2) for b in range(2)], axis=0))
        return jnp.concatenate(lined, axis=1)

    def double():
        return dot(stack_c[...], dup[...]).astype(BF16)

    for s, stack in ((0, stack_f), (1, stack_c)):
        n = streams[s].n
        got = narrow(streams[s], second[s], hb[s], zs[s])
        for r in range(streams[s].R):
            mixed = got(r) + inject[s][:, r, :].astype(F32)
            sl[s][:, r * streams[s].W : (r + 1) * streams[s].W] = mixed
            stack[r * n : (r + 1) * n, :] = mixed.astype(BF16)
    down = dot(rw[...], halve())
    wide = double()
    for R in range(c.R):
        lifted = dot(up[...], wide[R * c.n : (R + 1) * c.n, :])
        for r in (2 * R, 2 * R + 1):
            at = slice(r * f.W, (r + 1) * f.W)
            sl_f[:, at] = swish_derivative(sl_f[:, at] + lifted)
    sl_c[...] = swish_derivative(sl_c[...] + down)

    def total(field, k):
        for r in range(f.R):
            stack_f[r * f.n : (r + 1) * f.n, :] = (field(0, r) * own_row(0, sl_f, r)).astype(BF16)
        coarse_grads = [field(1, r) * own_row(1, sl_c, r) for r in range(c.R)]
        for r in range(c.R):
            stack_c[r * c.n : (r + 1) * c.n, :] = coarse_grads[r].astype(BF16)
        raised = dot(u4[...], halve())
        put_rows(c, [coarse_grads[r] + own_row(1, raised, r) for r in range(c.R)], xm_c.at[k], pk_c.at[k])
        wide = double()
        even = lanes_of((f.n, f.W)) % 2 == 0
        fine = []
        for R in range(c.R):
            spread_out = dot(rt[...], wide[R * c.n : (R + 1) * c.n, :])
            for a in range(2):
                part = [spread_out[(2 * a + b) * f.n : (2 * a + b + 1) * f.n] for b in range(2)]
                r = 2 * R + a
                fine.append(field(0, r) * own_row(0, sl_f, r) + jnp.where(even, part[0], part[1]))
        put_rows(f, fine, xm_f.at[k], pk_f.at[k])
        for s in both:
            exchange_start(s, k)

    total(lambda s, r: cot[s][:, r, :], TOTAL0)

    sums = []
    for s in both:
        load(s, TOTAL0, ring=False)
        widen(streams[s], a3[s], x3[s], x9[s], hg[s])

        def pushed(g, at, k):
            scaled = hg[s][at, block(k, 128)] * ls[s][at, block(k, 128)]
            return scaled, scaled * nm[s][at, block(k, 128)]

        sums.append(group_loop(s, *ring_chunks(s), 2, pushed))
    reduce_start(1, to_row(flat(sums, 0) + flat(sums, 1)))

    def scale(s, k):
        exchange_wait(s, k)
        load(s, k)
        widen(streams[s], a3[s], x3[s], x9[s], hg[s])

    for s in both:
        scale(s, TOTAL0)
    reduce_middle(1)
    along = []
    for s in both:

        def cot_sums(g, at, k):
            x = kc[s][at, block(k - streams[s].W // 128, 128)]
            return x, x * nm[s][at, block(k, 128)]

        along.append(group_loop(s, *own_chunks(s), 2, cot_sums))
    found = reduce_end(1)

    def image(row_sums):
        scaled_mean = row_sums * per
        got = []
        for s in both:
            gs = streams[s].gs
            for g in range(GROUPS):
                at = slice(g * gs, (g + 1) * gs)
                one, two = pick(scaled_mean, s * GROUPS + g), pick(scaled_mean, 8 + s * GROUPS + g)

                def centre(k, _):
                    here = block(k, 128)
                    scaled = hg[s][at, here] * ls[s][at, here]
                    grad = inverses[s][g] * (scaled - one - nm[s][at, here] * two)
                    hb[s][at, here] = (grad * mk[s][:, here]).astype(BF16)
                    return 0

                lax.fori_loop(0, streams[s].NL // 128, centre, 0)
            got.append(narrow(streams[s], a4[s], hb[s], zs[s]))
        return got

    got = image(found)
    for s in both:
        made = [got[s](r) for r in range(streams[s].R)]
        for r in range(streams[s].R):
            es[s][:, r * streams[s].W : (r + 1) * streams[s].W] = made[r]
        put_rows(streams[s], made, xm[s].at[IMAGE], pk[s].at[IMAGE])
        exchange_start(s, IMAGE)
    total(lambda s, r: own_row(s, es[s], r), TOTAL1)

    gram = [jnp.zeros((8, 128), F32) for _ in range(3)]
    for s in both:
        for r in range(streams[s].R):
            a, b = cot[s][:, r, :], own_row(s, es[s], r)
            for t, product in enumerate((a * a, a * b, b * b)):
                product = fold(product)
                for half in range(streams[s].W // 128):
                    gram[t] = gram[t] + product[:, half * 128 : (half + 1) * 128]
    sums = []
    crossed = [jnp.zeros((8, 128), F32) for _ in range(2)]
    for s in both:
        exchange_wait(s, IMAGE)
        load(s, IMAGE)
        widen(streams[s], a1[s], x3[s], x9[s], kp[s], inside=True)
    for s in both:
        scale(s, TOTAL1)

        def all_sums(g, at, k):
            here, inner = block(k, 128), block(k - streams[s].W // 128, 128)
            normed, lifted = nm[s][at, here], kp[s][at, inner]
            scaled = hg[s][at, here] * ls[s][at, here]
            return scaled, scaled * normed, lifted, lifted * normed, scaled * kc[s][at, inner], scaled * lifted

        sums.append(group_loop(s, *own_chunks(s), 6, all_sums))
        for g in range(GROUPS):
            for t in range(2):
                crossed[t] = crossed[t] + sums[s][4 + t][g] * inverses[s][g]
    entries = flat(sums, 0) + flat(sums, 1) + flat(along, 0) + flat(along, 1) + flat(sums, 2) + flat(sums, 3)
    reduce_start(2, to_row(entries + gram + crossed))
    reduce_middle(2)
    found = reduce_end(2)

    weight = (inverse_row + roll(inverse_row, 8)) * per
    cc, c0, g00, cq, pq = [pick(found, 48 + k) for k in range(5)]
    c1 = cq - jnp.sum(found * weight * roll(found, -16), axis=1, keepdims=True)
    g01 = pq - jnp.sum(found * weight * roll(found, -32), axis=1, keepdims=True)
    d0 = jnp.maximum(cc - c0, 0.25 * cc)
    alpha = 1.0 + c0 / d0
    kappa = alpha * g00 / d0
    turn = -alpha * (c1 - c0)
    d1 = jnp.maximum(-alpha * alpha * (g01 - g00) - kappa * alpha * (c1 - c0), 0.25 * alpha * alpha * g00)
    m0 = -((1.0 - alpha) * c0 + alpha * c1)
    m1 = -alpha * ((1.0 - alpha) * g00 + alpha * g01) + kappa * m0
    by0 = 1.0 - m0 / d0 + (m1 / d1) * (turn / d0)
    by1 = alpha * (1.0 - m1 / d1)

    got = image(found)
    for s in both:
        for r in range(streams[s].R):
            outs[s][:, r, :] = cot[s][:, r, :] + by0 * own_row(s, es[s], r) + by1 * got[s](r)

    for s in both:
        for k in range(5):
            exchange_end(s, k)
    for k in range(3):
        reduce_drain(k)


def solution(mesh):
    rows, cols = mesh.shape["row"], mesh.shape["col"]
    sizes = (rows, cols, min(rows, 8), min(cols, 4))

    def body(*args):
        fine_state, coarse_state = args[:2]
        fine_first, fine_second, coarse_first, coarse_second = args[6:10]
        f = Stream(fine_state.shape[0], fine_first.shape[1], *fine_state.shape[1:])
        c = Stream(coarse_state.shape[0], coarse_first.shape[1], *coarse_state.shape[1:])
        both = (f, c)
        args = list(args)
        for k, s in ((7, f), (9, c)):
            args[k] = args[k].reshape(3, 3 * s.n, s.w)
        for k in range(10, 14):
            args[k] = args[k].reshape(1, -1)
        vmem = pltpu.VMEM
        scratch = []
        for shape, dtype in (
            (lambda s: (5, s.n, (s.R + 4) * s.W), BF16),
            (lambda s: (5, s.n, 128), BF16),
            (lambda s: (5, 8, s.n, 128), BF16),
            (lambda s: (3 * s.n, (s.R + 4) * s.W), BF16),
            (lambda s: (3, 3 * s.n, 128), BF16),
            (lambda s: (s.w, s.NL), F32),
            (lambda s: (s.w, s.NL), F32),
            (lambda s: (s.w, s.NL), F32),
            (lambda s: (s.w, s.NL), BF16),
            (lambda s: (s.w, s.cells), F32),
            (lambda s: (s.w, s.cells), F32),
            (lambda s: (3 * s.n, s.cells), F32),
            (lambda s: (s.n, s.cells), F32),
            (lambda s: (s.n, s.cells), F32),
            (lambda s: (1, s.NL), F32),
            (lambda s: (s.w, 128), F32),
            (lambda s: (s.w, 128), F32),
            (lambda s: (3, s.w, 3 * s.n), BF16),
            (lambda s: (3, s.w, 3 * s.n), BF16),
            (lambda s: (3, 3 * s.n, s.w), BF16),
        ):
            scratch += [vmem(shape(s), dtype) for s in both]
        scratch += [
            vmem((128, 256), BF16),
            vmem((256, 256), BF16),
            vmem((4 * f.n, c.n), BF16),
            vmem((c.n, 4 * f.n), BF16),
            vmem((c.n, 4 * f.n), BF16),
            vmem((f.R * f.n, f.W), BF16),
            vmem((c.R * c.n, c.W), BF16),
            vmem((3 * c.n, c.w), BF16),
            vmem((3, sizes[2] * (cols // sizes[3]), 1, 128), F32),
            vmem((3, (rows // sizes[2]) * sizes[3], 1, 128), F32),
            pltpu.SemaphoreType.DMA((10, 10)),
            pltpu.SemaphoreType.DMA((10, 10)),
            pltpu.SemaphoreType.DMA((3, 2)),
            pltpu.SemaphoreType.DMA((3, 2)),
        ]
        return pl.pallas_call(
            functools.partial(kernel, both, sizes),
            out_shape=[jax.ShapeDtypeStruct(a.shape, F32) for a in args[4:6]],
            in_specs=[pl.BlockSpec(memory_space=pltpu.VMEM)] * 16,
            out_specs=[pl.BlockSpec(memory_space=pltpu.VMEM)] * 2,
            scratch_shapes=scratch,
            compiler_params=pltpu.CompilerParams(
                collective_id=0, has_side_effects=True, vmem_limit_bytes=56 * 1024 * 1024
            ),
        )(*args)

    field = P(None, "row", "col")
    return jax.shard_map(
        body,
        mesh=mesh,
        in_specs=(field,) * 6 + (P(),) * 10,
        out_specs=(field, field),
        check_vma=False,
    )
```

time: 889 us -> 107 us (0.12); the launches traced: 879 us -> 107 us
  blocking collectives: 532 us -> 0 us
  starting transfers between devices: 133 us -> 0 us
  Pallas kernels: 0 us -> 96.5 us
  waiting for transfers between devices: 67.8 us -> 0 us
  matrix products: 59.1 us -> 0 us
  other arithmetic: 33 us -> 0 us
  local copies, waits for them, and re-layouts: 35.7 us -> 9.4 us
  between operations: 18.8 us -> 0.66 us
    psum x6 -> x0, blocking collectives: 532 us -> none  [the longest x2 183 us: body(): grad_sums = lax.psum((local_grads[0], local_grads[1]), ('row', 'col'))]
    ppermute x48 -> x0, starting transfers between devices: 133 us -> none  [the longest x24 91.6 us: extended(): before = lax.ppermute(last, axis, up)]
    pallas_call x0 -> x1, Pallas kernels: none -> 96.5 us  [body(): pl.pallas_call(functools.partial(kernel, both, sizes), out_shape=[jax.Sha...]
    ppermute x48 -> x0, waiting for transfers between devices: 67.8 us -> none  [the longest x24 67.8 us: extended(): after = lax.ppermute(leading, axis, down)]
    dot_general x114 -> x0, matrix products: 59.1 us -> none  [the longest x72 38.2 us: conv_back(): jnp.einsum('oc,ohw->chw', weights[tap], window, preferred_element_type=jn...]
    reduce_sum x18 -> x0, other arithmetic: 11.6 us -> none  [the longest x4 5.29 us: inner(): return jnp.sum(first[0] * second[0]) + jnp.sum(first[1] * second[1])]
    convert_element_type x9 -> x0, other arithmetic: 10.3 us -> none  [the longest x2 3.72 us: body(): pre_grads[0].astype(jnp.bfloat16)]
  transfers between devices with their start and end apart: 48 -> 0, of which waited for: 4 -> 0; matrix products, arithmetic and copies ran while one was open for 7% -> 0% of each run, Pallas kernels for 0% -> 0%
where the time goes in v1:
time: 107 us
  Pallas kernels  96.5 us (90%)
  local copies, waits for them, and re-layouts  9.4 us (9%)
    pallas_call x1, Pallas kernels, body(): pl.pallas_call(functools.partial(kernel, both, sizes), out_shape=[jax.Sha...  96.5 us
    unnamed x9, local copies, waits for them, and re-layouts  6.83 us
    reshape x2, local copies, waits for them, and re-layouts, body(): args[k] = args[k].reshape(1, -1)  2.57 us

profile of v1, /device:TPU:1, one launch (start us, length us, event | category | flops | bytes accessed | tf_op | source)
XLA Modules:
  0.0 106.6 jit_solution(14560387548802777726)
XLA Ops:
  0.6 0.0 copy-start
  0.6 1.3 %reshape.26.refs_12_ = f32[1,320]{1,0:T(1,128)} reshape(f32[320]{0:T(512)} %param.28) | data formatting | bytes 2560 | tf_op jit(solution)/shard_map/reshape | solution.py:604
  1.9 1.3 %reshape.27.refs_13_ = f32[1,320]{1,0:T(1,128)} reshape(f32[320]{0:T(512)} %param.29) | data formatting | bytes 2560 | tf_op jit(solution)/shard_map/reshape | solution.py:604
  3.2 1.5 %copy.20.refs_14_ = bf16[2,2,64,32]{3,2,1,0:T(8,128)(2,1)} copy(bf16[2,2,64,32]{2,3,1,0:T(8,128)(2,1)} %param.30) | data formatting | bytes 32768 | tf_op args[14]
  4.7 1.8 %copy.18.refs_6_ = bf16[9,160,32]{2,1,0:T(8,128)(2,1)} copy(bf16[9,160,32]{1,2,0:T(8,128)(2,1)} %param.22) | data formatting | bytes 184320 | tf_op args[6]
  6.5 0.0 copy-done
  6.5 1.1 %copy.19.refs_8_ = bf16[9,320,64]{2,1,0:T(8,128)(2,1)} copy(bf16[9,320,64]{1,2,0:T(8,128)(2,1)S(1)} %copy-done) | data formatting | bytes 737280 | tf_op args[8]
  7.7 96.5 %shard_map.167 = (f32[32,8,256]{2,1,0:T(8,128)}, f32[64,4,128]{2,1,0:T(4,128)}) custom-call(bf16[32,8,256]{2,1,0:T(8,128)(2,1)} %refs_0_.1, bf16[64,4,128]{2,1,0:T(4,128)(2,1)} %refs_1_.1, bf16[32,8,256]{2,1,0:T(8,128)(2,1)} %refs_2_.1, bf16[64,4,128]{2,1,0:T(4,128)(2,1)} %refs_3_.1, f32[32,8,256]{2,1,0:T(8,128)} %refs_4_.1, f32[64,4,128]{2,1,0:T(4,128)} %refs_5_.1, ...), custom_call_target="tpu_custom_call" | custom-call | tf_op jit(solution)/shard_map/pallas_call | solution.py:646
  104.2 0.0 copy-start.1
  104.2 1.7 %copy.23 = f32[32,8,256]{2,1,0:T(8,128)} copy(f32[32,8,256]{2,1,0:T(8,128)} %get-tuple-element.4) | data formatting | bytes 524288
  105.9 0.0 copy-done.1
  105.9 0.7 copy.24
Async XLA Ops:
  0.6 5.9 %copy-start = (bf16[9,320,64]{1,2,0:T(8,128)(2,1)S(1)}, bf16[9,320,64]{1,2,0:T(8,128)(2,1)}, u32[]{:S(2)}) copy-start(bf16[9,320,64]{1,2,0:T(8,128)(2,1)} %param.24) | copy-start | bytes 1105924
  104.2 1.7 %copy-start.1 = (f32[64,4,128]{2,1,0:T(4,128)S(1)}, f32[64,4,128]{2,1,0:T(4,128)}, u32[]{:S(2)}) copy-start(f32[64,4,128]{2,1,0:T(4,128)} %get-tuple-element.5) | copy-start | bytes 393220

commit v2 on v1

--- a/solution.py
+++ b/solution.py
@@ -51,7 +51,7 @@
 
 
 def block(i, size):
-    return pl.ds(pl.multiple_of(i * size, 128), size)
+    return slice(i * size, (i + 1) * size)
 
 
 def swish_derivative(v):
@@ -125,31 +125,21 @@
 
 
 def widen(s, weights, x3, x9, out, inside=False):
-    skip = s.W if inside else 0
-
-    def step(b, _):
-        total = dot(weights[0], x3[:, pl.ds(pl.multiple_of(b * 256 + skip, 128), 256)])
-        for i in (1, 2):
-            total = total + dot(weights[i], x3[:, pl.ds(pl.multiple_of(b * 256 + skip + i * s.W, 128), 256)])
-        out[:, block(b, 256)] = total
-        return 0
-
-    lax.fori_loop(0, (s.cells if inside else s.main) // 256, step, 0)
+    start, size = (s.W, s.cells) if inside else (0, s.main)
+    taps = [x3[:, start + i * s.W : start + i * s.W + size] for i in range(3)]
+    out[:, 0:size] = dot(weights[...], jnp.concatenate(taps, axis=0))
     if not inside:
-        out[:, s.main :] = dot(weights[0], x9[0]) + dot(weights[1], x9[1]) + dot(weights[2], x9[2])
+        out[:, s.main :] = dot(weights[...], jnp.concatenate([x9[i] for i in range(3)], axis=0))
 
 
 def narrow(s, weights, h, z):
     n, W = s.n, s.W
 
-    def step(b, _):
-        total = dot(weights[0], h[:, block(b, 256)])
+    for b in range(0, s.cells, 256):
+        total = dot(weights[0], h[:, b : b + 256])
         for i in (1, 2):
-            total = total + dot(weights[i], h[:, pl.ds(pl.multiple_of(b * 256 + i * W, 128), 256)])
-        z[:, block(b, 256)] = total
-        return 0
-
-    lax.fori_loop(0, s.cells // 256, step, 0)
+            total = total + dot(weights[i], h[:, b + i * W : b + i * W + 256])
+        z[:, b : b + 256] = total
     edges = [dot(weights[i], h[:, s.main :]) for i in range(3)]
     total = edges[0] + roll(edges[1], -8) + roll(edges[2], -16)
     q = lanes_of((n, 128)) % 8
@@ -309,20 +299,15 @@
 
     for s in both:
         n, w, W = streams[s].n, streams[s].w, streams[s].W
-        for i in range(3):
-            flipped = []
-            for j in range(3):
-                tap = first[s][3 * i + j].T
-                taps[j * n : (j + 1) * n, 0:w] = tap
-                a4[s][2 - i, (2 - j) * n : (3 - j) * n, :] = tap
-            a1[s][i] = taps[0 : 3 * n, 0:w].T
-            for j in range(3):
-                t = 8 - (3 * i + j)
-                taps[j * n : (j + 1) * n, 0:w] = second[s][t // 3, (t % 3) * n : (t % 3 + 1) * n, :]
-            a3[s][i] = taps[0 : 3 * n, 0:w].T
+        for t in range(9):
+            back = slice((8 - t) * n, (9 - t) * n)
+            a4[s][(8 - t) // 3, (8 - t) % 3 * n : ((8 - t) % 3 + 1) * n, :] = first[s][t * n : (t + 1) * n, :]
+            taps[back, 0:w] = second[s][t // 3, (t % 3) * n : (t % 3 + 1) * n, :]
+        a1[s][...] = first[s][...].T
+        a3[s][...] = taps[0 : 9 * n, 0:w].T
         same = subs_of((w, w)) == lanes_of((w, w))
         for src, dst in (((fine_gain, coarse_gain)[s], ga[s]), ((fine_shift, coarse_shift)[s], sh[s])):
-            dst[...] = jnp.broadcast_to(jnp.sum(jnp.where(same, src[...], 0.0), axis=1, keepdims=True), (w, 128))
+            dst[...] = jnp.broadcast_to(jnp.sum(jnp.where(same, src[...][None, :], 0.0), axis=1, keepdims=True), (w, 128))
         R = streams[s].R
         mk[s][...] = jnp.ones((1, streams[s].NL), F32)
         mk[s][:, 0:W] = jnp.where(row > 0, 1.0, 0.0) * jnp.ones((1, W), F32)
@@ -339,7 +324,7 @@
     for a in range(2):
         for b in range(2):
             at = slice((2 * a + b) * f.n, (2 * a + b + 1) * f.n)
-            rt[at, :] = reduction[a, b].T
+            rt[at, :] = reduction[at, :]
             taps[at, 0 : c.n] = up[...]
     rw[...] = rt[...].T
     u4[...] = taps[0 : 4 * f.n, 0 : c.n].T
@@ -355,10 +340,10 @@
         for g in range(GROUPS):
             at = slice(g * gs, (g + 1) * gs)
 
-            def step(k, accs):
-                return tuple(a + fold(t) for a, t in zip(accs, body(g, at, k + start)))
-
-            sums.append(lax.fori_loop(0, chunks, step, (jnp.zeros((8, 128), F32),) * count))
+            accs = [jnp.zeros((8, 128), F32)] * count
+            for k in range(start, start + chunks):
+                accs = [a + fold(t) for a, t in zip(accs, body(g, at, k))]
+            sums.append(accs)
         return [[sums[g][t] for g in range(GROUPS)] for t in range(count)]
 
     def ring_chunks(s):
@@ -403,7 +388,7 @@
         for g in range(GROUPS):
             at = slice(g * gs, (g + 1) * gs)
 
-            def activate(k, _):
+            for k in range(streams[s].NL // 128):
                 here = block(k, 128)
                 gain, keep = ga[s][at, :], mk[s][:, here]
                 normed = (nm[s][at, here] - means[s][g]) * inverses[s][g]
@@ -412,9 +397,6 @@
                 nm[s][at, here] = normed
                 hb[s][at, here] = (level * sigma * keep).astype(BF16)
                 ls[s][at, here] = sigma * (1.0 + level * (1.0 - sigma)) * gain * keep
-                return 0
-
-            lax.fori_loop(0, streams[s].NL // 128, activate, 0)
 
     def own_row(s, ref, r):
         return ref[:, r * streams[s].W : (r + 1) * streams[s].W]
@@ -509,14 +491,11 @@
                 at = slice(g * gs, (g + 1) * gs)
                 one, two = pick(scaled_mean, s * GROUPS + g), pick(scaled_mean, 8 + s * GROUPS + g)
 
-                def centre(k, _):
+                for k in range(streams[s].NL // 128):
                     here = block(k, 128)
                     scaled = hg[s][at, here] * ls[s][at, here]
                     grad = inverses[s][g] * (scaled - one - nm[s][at, here] * two)
                     hb[s][at, here] = (grad * mk[s][:, here]).astype(BF16)
-                    return 0
-
-                lax.fori_loop(0, streams[s].NL // 128, centre, 0)
             got.append(narrow(streams[s], a4[s], hb[s], zs[s]))
         return got
 
@@ -598,10 +577,10 @@
         c = Stream(coarse_state.shape[0], coarse_first.shape[1], *coarse_state.shape[1:])
         both = (f, c)
         args = list(args)
-        for k, s in ((7, f), (9, c)):
-            args[k] = args[k].reshape(3, 3 * s.n, s.w)
-        for k in range(10, 14):
-            args[k] = args[k].reshape(1, -1)
+        for k, s in ((6, f), (8, c)):
+            args[k] = args[k].transpose(0, 2, 1).reshape(9 * s.n, s.w)
+            args[k + 1] = args[k + 1].reshape(3, 3 * s.n, s.w)
+        args[14] = args[14].transpose(0, 1, 3, 2).reshape(4 * f.n, c.n)
         vmem = pltpu.VMEM
         scratch = []
         for shape, dtype in (
@@ -622,8 +601,8 @@
             (lambda s: (1, s.NL), F32),
             (lambda s: (s.w, 128), F32),
             (lambda s: (s.w, 128), F32),
-            (lambda s: (3, s.w, 3 * s.n), BF16),
-            (lambda s: (3, s.w, 3 * s.n), BF16),
+            (lambda s: (s.w, 9 * s.n), BF16),
+            (lambda s: (s.w, 9 * s.n), BF16),
             (lambda s: (3, 3 * s.n, s.w), BF16),
         ):
             scratch += [vmem(shape(s), dtype) for s in both]
@@ -635,7 +614,7 @@
             vmem((c.n, 4 * f.n), BF16),
             vmem((f.R * f.n, f.W), BF16),
             vmem((c.R * c.n, c.W), BF16),
-            vmem((3 * c.n, c.w), BF16),
+            vmem((9 * c.n, c.w), BF16),
             vmem((3, sizes[2] * (cols // sizes[3]), 1, 128), F32),
             vmem((3, (rows // sizes[2]) * sizes[3], 1, 128), F32),
             pltpu.SemaphoreType.DMA((10, 10)),

time: 107 us -> 83.4 us (0.78)
  Pallas kernels: 96.5 us -> 79.8 us
  local copies, waits for them, and re-layouts: 9.4 us -> 2.36 us
    pallas_call x1, Pallas kernels: 96.5 us -> 79.8 us  [body(): pl.pallas_call(functools.partial(kernel, both, sizes), out_shape=[jax.Sha...]
    unnamed x9 -> x4, local copies, waits for them, and re-layouts: 6.83 us -> 2.36 us
    reshape x2 -> x0, local copies, waits for them, and re-layouts: 2.57 us -> none  [body(): args[k] = args[k].reshape(1, -1)]
where the time goes in v2:
time: 83.4 us; the launch traced here: 82.9 us
  Pallas kernels  79.8 us (96%)
  local copies, waits for them, and re-layouts  2.36 us (3%)
    pallas_call x1, Pallas kernels, body(): pl.pallas_call(functools.partial(kernel, both, sizes), out_shape=[jax.Sha...  79.8 us
    unnamed x4, local copies, waits for them, and re-layouts  2.36 us

profile of v2, /device:TPU:1, one launch (start us, length us, event | category | flops | bytes accessed | tf_op | source)
XLA Modules:
  0.0 82.9 jit_solution(5607668018312131761)
XLA Ops:
  0.6 79.8 %shard_map.167 = (f32[32,8,256]{2,1,0:T(8,128)}, f32[64,4,128]{2,1,0:T(4,128)}) custom-call(bf16[32,8,256]{2,1,0:T(8,128)(2,1)} %refs_0_.1, bf16[64,4,128]{2,1,0:T(4,128)(2,1)} %refs_1_.1, bf16[32,8,256]{2,1,0:T(8,128)(2,1)} %refs_2_.1, bf16[64,4,128]{2,1,0:T(4,128)(2,1)} %refs_3_.1, f32[32,8,256]{2,1,0:T(8,128)} %refs_4_.1, f32[64,4,128]{2,1,0:T(4,128)} %refs_5_.1, ...), custom_call_target="tpu_custom_call" | custom-call | tf_op jit(solution)/shard_map/pallas_call | solution.py:625
  80.5 0.0 copy-start
  80.5 1.7 %copy.20 = f32[32,8,256]{2,1,0:T(8,128)} copy(f32[32,8,256]{2,1,0:T(8,128)} %get-tuple-element.4) | data formatting | bytes 524288
  82.2 0.0 copy-done
  82.2 0.7 copy.21
Async XLA Ops:
  80.5 1.7 %copy-start = (f32[64,4,128]{2,1,0:T(4,128)S(1)}, f32[64,4,128]{2,1,0:T(4,128)}, u32[]{:S(2)}) copy-start(f32[64,4,128]{2,1,0:T(4,128)} %get-tuple-element.5) | copy-start | bytes 393220

commit v3 on v2

--- a/solution.py
+++ b/solution.py
@@ -13,7 +13,9 @@
 F32 = jnp.float32
 BF16 = jnp.bfloat16
 DIRS = [(dr, dc) for dr in (-1, 0, 1) for dc in (-1, 0, 1) if dr or dc]
-STATE, COT, TOTAL0, TOTAL1, IMAGE = range(5)
+DIAGONALS = [(-1, -1), (-1, 1), (1, -1), (1, 1)]
+STATE, TOTAL0, TOTAL1, COT, IMAGE = range(5)
+SENT = 3
 
 
 class Stream:
@@ -75,32 +77,19 @@
     return jnp.sum(jnp.where(lanes_of((1, 128)) == k, row, 0.0), axis=1, keepdims=True)
 
 
-def put_rows(s, rows, xm, pk):
+def put_rows(s, rows, xm):
+    for r, x in enumerate(rows):
+        xm[:, (r + 2) * s.W : (r + 3) * s.W] = x.astype(BF16)
+
+
+def pack(s, xm, lines):
     lane = lanes_of((s.n, 128))
     packed = jnp.zeros((s.n, 128), F32)
-    for r, x in enumerate(rows):
-        xm[:, (r + 2) * s.W : (r + 3) * s.W] = x.astype(BF16)
-        x = x.astype(F32)
-        edge = jnp.where(lane < 2, x[:, :128], jnp.where(lane >= 126, x[:, s.W - 128 :], 0.0))
-        packed = packed + roll(edge, 8 * (r + 2) + 2)
-    pk[...] = jnp.where(lane % 8 <= 2, packed, roll(packed, 2)).astype(BF16)
-
-
-def edge_of(s, pk, pr):
-    lane = lanes_of((s.n, 128))
-    q = lane % 8
-
-    def across(left, mid, right):
-        return jnp.where(q <= 1, left, jnp.where(q <= 3, mid, right))
-
-    own = (lane >= 16) & (lane < 16 + 8 * s.R)
-    if pr is None:
-        return jnp.where(own & (q >= 2) & (q <= 3), pk[...].astype(F32), 0.0)
-    got = {d: pr[k].astype(F32) for k, d in enumerate(DIRS)}
-    mid = across(got[0, -1], pk[...].astype(F32), got[0, 1])
-    top = across(got[-1, -1], got[-1, 0], got[-1, 1])
-    bottom = across(got[1, -1], got[1, 0], got[1, 1])
-    return jnp.where(own, mid, jnp.where(lane < 16, roll(top, -8 * s.R), roll(bottom, 8 * s.R)))
+    for k in lines:
+        left, right = xm[:, k * s.W : k * s.W + 128], xm[:, (k + 1) * s.W - 128 : (k + 1) * s.W]
+        x = jnp.where(lane < 2, left.astype(F32), jnp.where(lane >= 126, right.astype(F32), 0.0))
+        packed = packed + roll(x, 8 * k + 2)
+    return jnp.where(lane % 8 <= 2, packed, roll(packed, 2))
 
 
 def build(s, xm, edge, x3, x9, ring):
@@ -124,12 +113,10 @@
             x9[i, j * n : (j + 1) * n, :] = roll(edge, -(8 * i + j)).astype(BF16)
 
 
-def widen(s, weights, x3, x9, out, inside=False):
-    start, size = (s.W, s.cells) if inside else (0, s.main)
-    taps = [x3[:, start + i * s.W : start + i * s.W + size] for i in range(3)]
-    out[:, 0:size] = dot(weights[...], jnp.concatenate(taps, axis=0))
-    if not inside:
-        out[:, s.main :] = dot(weights[...], jnp.concatenate([x9[i] for i in range(3)], axis=0))
+def widen(s, weights, x3, x9, out):
+    taps = [x3[:, i * s.W : i * s.W + s.main] for i in range(3)]
+    out[:, 0 : s.main] = dot(weights[...], jnp.concatenate(taps, axis=0))
+    out[:, s.main :] = dot(weights[...], jnp.concatenate([x9[i] for i in range(3)], axis=0))
 
 
 def narrow(s, weights, h, z):
@@ -165,12 +152,12 @@
         fine_out, coarse_out,
         *rest,
     ) = refs
-    (xm_f, xm_c, pk_f, pk_c, pr_f, pr_c, x3_f, x3_c, x9_f, x9_c,
+    (xm_f, xm_c, x3_f, x3_c, x9_f, x9_c,
      nm_f, nm_c, ls_f, ls_c, hg_f, hg_c, hb_f, hb_c, kc_f, kc_c, kp_f, kp_c,
      z_f, z_c, sl_f, sl_c, e_f, e_c, mk_f, mk_c, ga_f, ga_c, sh_f, sh_c,
      a1_f, a1_c, a3_f, a3_c, a4_f, a4_c, dup, split, rt, rw, u4, stack_f, stack_c, taps,
-     ar_a, ar_b, halo_send, halo_recv, ar_send, ar_recv) = rest
-    xm, pk, pr, x3, x9 = (xm_f, xm_c), (pk_f, pk_c), (pr_f, pr_c), (x3_f, x3_c), (x9_f, x9_c)
+     pk, pr, corner, corners, ar_a, ar_b, halo_send, halo_recv, ar_send, ar_recv) = rest
+    xm, x3, x9 = (xm_f, xm_c), (x3_f, x3_c), (x9_f, x9_c)
     nm, ls, hg, hb = (nm_f, nm_c), (ls_f, ls_c), (hg_f, hg_c), (hb_f, hb_c)
     kc, kp, zs, sl, es, mk = (kc_f, kc_c), (kp_f, kp_c), (z_f, z_c), (sl_f, sl_c), (e_f, e_c), (mk_f, mk_c)
     ga, sh, a1, a3, a4 = (ga_f, ga_c), (sh_f, sh_c), (a1_f, a1_c), (a3_f, a3_c), (a4_f, a4_c)
@@ -181,6 +168,7 @@
     high_rows, high_cols = rows // low_rows, cols // low_cols
     row, col = lax.axis_index("row"), lax.axis_index("col")
     both = (0, 1)
+    own_part = (slice(0, f.n), slice(f.n, f.n + c.n))
 
     def has(d):
         return (row + d[0] >= 0) & (row + d[0] < rows) & (col + d[1] >= 0) & (col + d[1] < cols)
@@ -197,39 +185,88 @@
         p = (me_b + k) % size_b
         return ((p // low_cols) * low_rows + row % low_rows, (col // low_cols) * low_cols + p % low_cols)
 
-    def exchange_copies(s, k):
-        W, R = streams[s].W, streams[s].R
-        field = 2 * k + s
+    def strips(k):
         made = []
-        for i, d in enumerate(DIRS):
-            back = DIRS.index((-d[0], -d[1]))
+        for s in both:
+            W, R = streams[s].W, streams[s].R
+            for i, d, src, dst in ((s, (-1, 0), 2 * W, (R + 2) * W), (2 + s, (1, 0), R * W, 0)):
+                made.append((pltpu.make_async_remote_copy(
+                    src_ref=xm[s].at[k, :, pl.ds(src, 2 * W)], dst_ref=xm[s].at[k, :, pl.ds(dst, 2 * W)],
+                    send_sem=halo_send.at[k, i], recv_sem=halo_recv.at[k, i],
+                    device_id=(row + d[0], col), device_id_type=MESH), d))
+        return made
+
+    def packs(k):
+        made = []
+        for i, dc in ((4, -1), (5, 1)):
             made.append((pltpu.make_async_remote_copy(
-                src_ref=pk[s].at[k], dst_ref=pr[s].at[k, back],
-                send_sem=halo_send.at[field, i], recv_sem=halo_recv.at[field, back],
-                device_id=(row + d[0], col + d[1]), device_id_type=MESH), d))
-        for i, d, src, dst in ((8, (-1, 0), 2 * W, (R + 2) * W), (9, (1, 0), R * W, 0)):
+                src_ref=pk.at[k], dst_ref=pr.at[k, i - 4],
+                send_sem=halo_send.at[k, i], recv_sem=halo_recv.at[k, i],
+                device_id=(row, col + dc), device_id_type=MESH), (0, dc)))
+        for i, (dr, dc) in enumerate(DIAGONALS):
             made.append((pltpu.make_async_remote_copy(
-                src_ref=xm[s].at[k, :, pl.ds(src, 2 * W)], dst_ref=xm[s].at[k, :, pl.ds(dst, 2 * W)],
-                send_sem=halo_send.at[field, i], recv_sem=halo_recv.at[field, i],
-                device_id=(row + d[0], col), device_id_type=MESH), d))
+                src_ref=corner.at[k, (dr + 1) // 2], dst_ref=corners.at[k, i],
+                send_sem=halo_send.at[k, 6 + i], recv_sem=halo_recv.at[k, 6 + i],
+                device_id=(row + dr, col + dc), device_id_type=MESH), (dr, dc)))
         return made
 
-    def exchange_start(s, k):
-        for copy, d in exchange_copies(s, k):
+    def pack_own(k):
+        for s in both:
+            R = streams[s].R
+            pk[k, own_part[s], :] = pack(streams[s], xm[s].at[k], range(2, R + 2)).astype(BF16)
+
+    def exchange_start(k):
+        for copy, d in strips(k):
             pl.when(has(d))(copy.start)
-
-    def exchange_wait(s, k):
-        W, R = streams[s].W, streams[s].R
-        field = 2 * k + s
-        for i, d in enumerate(DIRS):
-            pl.when(has(d))(pltpu.make_async_copy(pk[s].at[k], pr[s].at[k, i], halo_recv.at[field, i]).wait)
-        for i, d, dst in ((8, (1, 0), (R + 2) * W), (9, (-1, 0), 0)):
-            ref = xm[s].at[k, :, pl.ds(dst, 2 * W)]
-            pl.when(has(d))(pltpu.make_async_copy(ref, ref, halo_recv.at[field, i]).wait)
-
-    def exchange_end(s, k):
-        for copy, d in exchange_copies(s, k):
+        pack_own(k)
+        own = pk[k].astype(F32)
+        shift = 8 * (f.R - c.R)
+        low = jnp.concatenate([own[: f.n], roll(own[f.n :], shift)], axis=0)
+        lane = lanes_of(own.shape)
+        cells = jnp.where(lane < 8 * (c.R + 2), own, low)
+        cells = jnp.concatenate([cells, jnp.zeros((128 - f.n - c.n, 128), F32)], axis=0).T
+        corner[k, 0] = cells[16:32].astype(BF16)
+        corner[k, 1] = cells[8 * f.R : 8 * f.R + 16].astype(BF16)
+        for copy, d in packs(k):
+            pl.when(has(d))(copy.start)
+
+    def exchange_wait(k):
+        for copy, d in strips(k) + packs(k):
+            pl.when(has((-d[0], -d[1])))(copy.wait_recv)
+
+    def exchange_end(k):
+        for copy, d in strips(k) + packs(k):
             pl.when(has(d))(copy.wait_send)
+
+    def edges(k, ring):
+        lane = lanes_of((f.n + c.n, 128))
+        q = lane % 8
+        own = pk[k].astype(F32)
+        if ring:
+            sides = jnp.where(q <= 1, pr[k, 1].astype(F32), jnp.where(q <= 3, own, pr[k, 0].astype(F32)))
+            sub = subs_of((16, 128)) % 8
+            got = [corners[k, i].astype(F32) for i in range(4)]
+            above = jnp.where(sub <= 3, got[DIAGONALS.index((1, 1))], got[DIAGONALS.index((1, -1))])
+            below = jnp.where(sub <= 3, got[DIAGONALS.index((-1, 1))], got[DIAGONALS.index((-1, -1))])
+            low = 8 * (f.R + 2)
+            blank = [jnp.zeros((low - 16, 128), F32), jnp.zeros((112 - low, 128), F32)]
+            cells = jnp.concatenate([above, blank[0], below, blank[1]], axis=0).T
+        else:
+            sides = jnp.where((q >= 2) & (q <= 3), own, 0.0)
+        made = []
+        for s in both:
+            n, R = streams[s].n, streams[s].R
+            lane = lanes_of((n, 128))
+            q = lane % 8
+            outside = jnp.zeros((n, 128), F32)
+            if ring:
+                outer = cells[own_part[s]]
+                outer = jnp.where(lane < 16, outer, roll(outer, 8 * (R - f.R)))
+                lines = pack(streams[s], xm[s].at[k], (0, 1, R + 2, R + 3))
+                outside = jnp.where((q >= 2) & (q <= 3), lines, outer)
+            inside = (lane >= 16) & (lane < 16 + 8 * R)
+            made.append(jnp.where(inside, sides[own_part[s]], outside))
+        return made
 
     def spread(k, stage, buf, me, size, peer):
         def send(p, _):
@@ -264,10 +301,11 @@
 
     for s in both:
         W, R = streams[s].W, streams[s].R
-        for k in range(5):
-            pr[s][k] = jnp.zeros(pr[s].shape[1:], BF16)
+        for k in range(SENT):
             xm[s][k, :, 0 : 2 * W] = jnp.zeros((streams[s].n, 2 * W), BF16)
             xm[s][k, :, (R + 2) * W : (R + 4) * W] = jnp.zeros((streams[s].n, 2 * W), BF16)
+    pr[...] = jnp.zeros(pr.shape, BF16)
+    corners[...] = jnp.zeros(corners.shape, BF16)
     barrier = pltpu.get_barrier_semaphore()
 
     def greet(device):
@@ -287,15 +325,13 @@
     lax.fori_loop(1, size_a, greet_a, 0)
     lax.fori_loop(1, size_b, greet_b, 0)
     for s in both:
-        put_rows(streams[s], [state[s][:, r, :].astype(F32) for r in range(streams[s].R)], xm[s].at[STATE], pk[s].at[STATE])
+        put_rows(streams[s], [state[s][:, r, :] for r in range(streams[s].R)], xm[s].at[STATE])
     beside = sum(has(d).astype(jnp.int32) for d in DIRS)
     pl.semaphore_wait(barrier, beside + (size_a + size_b - 2))
-    for s in both:
-        exchange_start(s, STATE)
-    for s in both:
-        put_rows(streams[s], [cot[s][:, r, :] for r in range(streams[s].R)], xm[s].at[COT], pk[s].at[COT])
-    for s in both:
-        exchange_start(s, COT)
+    exchange_start(STATE)
+    for s in both:
+        put_rows(streams[s], [cot[s][:, r, :] for r in range(streams[s].R)], xm[s].at[COT])
+    pack_own(COT)
 
     for s in both:
         n, w, W = streams[s].n, streams[s].w, streams[s].W
@@ -329,10 +365,17 @@
     rw[...] = rt[...].T
     u4[...] = taps[0 : 4 * f.n, 0 : c.n].T
 
-    def load(s, k, ring=True):
-        st = streams[s]
-        edge = edge_of(st, pk[s].at[k], pr[s].at[k] if ring else None)
-        build(st, xm[s].at[k], edge, x3[s], x9[s], ring)
+    def spread_wide(k, weights, outs, ring=True):
+        if ring:
+            exchange_wait(k)
+        tiles = edges(k, ring)
+        for s in both:
+            build(streams[s], xm[s].at[k], tiles[s], x3[s], x9[s], ring)
+            widen(streams[s], weights[s], x3[s], x9[s], outs[s])
+
+    def masked(s, k, x):
+        W, R = streams[s].W, streams[s].R
+        return x if W <= 128 * k < (R + 1) * W else x * mk[s][:, block(k, 128)]
 
     def group_loop(s, start, chunks, count, body):
         gs = streams[s].gs
@@ -356,10 +399,8 @@
         return [a for s in both for a in per_stream[s][t]]
 
     sums = []
-    for s in both:
-        exchange_wait(s, STATE)
-        load(s, STATE)
-        widen(streams[s], a1[s], x3[s], x9[s], nm[s])
+    spread_wide(STATE, a1, nm)
+    for s in both:
 
         def squares(g, at, k):
             x = nm[s][at, block(k, 128)]
@@ -367,10 +408,7 @@
 
         sums.append(group_loop(s, *own_chunks(s), 2, squares))
     reduce_start(0, to_row(flat(sums, 0) + flat(sums, 1)))
-    for s in both:
-        exchange_wait(s, COT)
-        load(s, COT)
-        widen(streams[s], a1[s], x3[s], x9[s], kc[s], inside=True)
+    spread_wide(COT, a1, kc, ring=False)
     reduce_middle(0)
     stats = reduce_end(0)
 
@@ -436,7 +474,7 @@
         for r in range(c.R):
             stack_c[r * c.n : (r + 1) * c.n, :] = coarse_grads[r].astype(BF16)
         raised = dot(u4[...], halve())
-        put_rows(c, [coarse_grads[r] + own_row(1, raised, r) for r in range(c.R)], xm_c.at[k], pk_c.at[k])
+        put_rows(c, [coarse_grads[r] + own_row(1, raised, r) for r in range(c.R)], xm_c.at[k])
         wide = double()
         even = lanes_of((f.n, f.W)) % 2 == 0
         fine = []
@@ -446,16 +484,14 @@
                 part = [spread_out[(2 * a + b) * f.n : (2 * a + b + 1) * f.n] for b in range(2)]
                 r = 2 * R + a
                 fine.append(field(0, r) * own_row(0, sl_f, r) + jnp.where(even, part[0], part[1]))
-        put_rows(f, fine, xm_f.at[k], pk_f.at[k])
-        for s in both:
-            exchange_start(s, k)
+        put_rows(f, fine, xm_f.at[k])
+        exchange_start(k)
 
     total(lambda s, r: cot[s][:, r, :], TOTAL0)
 
     sums = []
-    for s in both:
-        load(s, TOTAL0, ring=False)
-        widen(streams[s], a3[s], x3[s], x9[s], hg[s])
+    spread_wide(TOTAL0, a3, hg, ring=False)
+    for s in both:
 
         def pushed(g, at, k):
             scaled = hg[s][at, block(k, 128)] * ls[s][at, block(k, 128)]
@@ -464,22 +500,16 @@
         sums.append(group_loop(s, *ring_chunks(s), 2, pushed))
     reduce_start(1, to_row(flat(sums, 0) + flat(sums, 1)))
 
-    def scale(s, k):
-        exchange_wait(s, k)
-        load(s, k)
-        widen(streams[s], a3[s], x3[s], x9[s], hg[s])
-
-    for s in both:
-        scale(s, TOTAL0)
+    spread_wide(TOTAL0, a3, hg)
     reduce_middle(1)
     along = []
     for s in both:
 
         def cot_sums(g, at, k):
-            x = kc[s][at, block(k - streams[s].W // 128, 128)]
+            x = masked(s, k, kc[s][at, block(k, 128)])
             return x, x * nm[s][at, block(k, 128)]
 
-        along.append(group_loop(s, *own_chunks(s), 2, cot_sums))
+        along.append(group_loop(s, *ring_chunks(s), 2, cot_sums))
     found = reduce_end(1)
 
     def image(row_sums):
@@ -504,8 +534,7 @@
         made = [got[s](r) for r in range(streams[s].R)]
         for r in range(streams[s].R):
             es[s][:, r * streams[s].W : (r + 1) * streams[s].W] = made[r]
-        put_rows(streams[s], made, xm[s].at[IMAGE], pk[s].at[IMAGE])
-        exchange_start(s, IMAGE)
+        put_rows(streams[s], made, xm[s].at[IMAGE])
     total(lambda s, r: own_row(s, es[s], r), TOTAL1)
 
     gram = [jnp.zeros((8, 128), F32) for _ in range(3)]
@@ -516,26 +545,37 @@
                 product = fold(product)
                 for half in range(streams[s].W // 128):
                     gram[t] = gram[t] + product[:, half * 128 : (half + 1) * 128]
-    sums = []
+    pack_own(IMAGE)
+    spread_wide(IMAGE, a1, kp, ring=False)
+    image_sums = []
+    for s in both:
+
+        def lifted_sums(g, at, k):
+            x = masked(s, k, kp[s][at, block(k, 128)])
+            return x, x * nm[s][at, block(k, 128)]
+
+        image_sums.append(group_loop(s, *ring_chunks(s), 2, lifted_sums))
+    spread_wide(TOTAL1, a3, hg)
+    sums, pairs = [], []
     crossed = [jnp.zeros((8, 128), F32) for _ in range(2)]
     for s in both:
-        exchange_wait(s, IMAGE)
-        load(s, IMAGE)
-        widen(streams[s], a1[s], x3[s], x9[s], kp[s], inside=True)
-    for s in both:
-        scale(s, TOTAL1)
-
-        def all_sums(g, at, k):
-            here, inner = block(k, 128), block(k - streams[s].W // 128, 128)
-            normed, lifted = nm[s][at, here], kp[s][at, inner]
+
+        def own_sums(g, at, k):
+            here = block(k, 128)
             scaled = hg[s][at, here] * ls[s][at, here]
-            return scaled, scaled * normed, lifted, lifted * normed, scaled * kc[s][at, inner], scaled * lifted
-
-        sums.append(group_loop(s, *own_chunks(s), 6, all_sums))
+            return scaled, scaled * nm[s][at, here]
+
+        def pair_sums(g, at, k):
+            here = block(k, 128)
+            scaled = hg[s][at, here] * ls[s][at, here]
+            return scaled * kc[s][at, here], scaled * kp[s][at, here]
+
+        sums.append(group_loop(s, *own_chunks(s), 2, own_sums))
+        pairs.append(group_loop(s, *ring_chunks(s), 2, pair_sums))
         for g in range(GROUPS):
             for t in range(2):
-                crossed[t] = crossed[t] + sums[s][4 + t][g] * inverses[s][g]
-    entries = flat(sums, 0) + flat(sums, 1) + flat(along, 0) + flat(along, 1) + flat(sums, 2) + flat(sums, 3)
+                crossed[t] = crossed[t] + pairs[s][t][g] * inverses[s][g]
+    entries = flat(sums, 0) + flat(sums, 1) + flat(along, 0) + flat(along, 1) + flat(image_sums, 0) + flat(image_sums, 1)
     reduce_start(2, to_row(entries + gram + crossed))
     reduce_middle(2)
     found = reduce_end(2)
@@ -559,9 +599,8 @@
         for r in range(streams[s].R):
             outs[s][:, r, :] = cot[s][:, r, :] + by0 * own_row(s, es[s], r) + by1 * got[s](r)
 
-    for s in both:
-        for k in range(5):
-            exchange_end(s, k)
+    for k in range(SENT):
+        exchange_end(k)
     for k in range(3):
         reduce_drain(k)
 
@@ -585,16 +624,14 @@
         scratch = []
         for shape, dtype in (
             (lambda s: (5, s.n, (s.R + 4) * s.W), BF16),
-            (lambda s: (5, s.n, 128), BF16),
-            (lambda s: (5, 8, s.n, 128), BF16),
             (lambda s: (3 * s.n, (s.R + 4) * s.W), BF16),
             (lambda s: (3, 3 * s.n, 128), BF16),
             (lambda s: (s.w, s.NL), F32),
             (lambda s: (s.w, s.NL), F32),
             (lambda s: (s.w, s.NL), F32),
             (lambda s: (s.w, s.NL), BF16),
-            (lambda s: (s.w, s.cells), F32),
-            (lambda s: (s.w, s.cells), F32),
+            (lambda s: (s.w, s.NL), F32),
+            (lambda s: (s.w, s.NL), F32),
             (lambda s: (3 * s.n, s.cells), F32),
             (lambda s: (s.n, s.cells), F32),
             (lambda s: (s.n, s.cells), F32),
@@ -615,10 +652,14 @@
             vmem((f.R * f.n, f.W), BF16),
             vmem((c.R * c.n, c.W), BF16),
             vmem((9 * c.n, c.w), BF16),
+            vmem((5, f.n + c.n, 128), BF16),
+            vmem((SENT, 2, f.n + c.n, 128), BF16),
+            vmem((SENT, 2, 16, 128), BF16),
+            vmem((SENT, 4, 16, 128), BF16),
             vmem((3, sizes[2] * (cols // sizes[3]), 1, 128), F32),
             vmem((3, (rows // sizes[2]) * sizes[3], 1, 128), F32),
-            pltpu.SemaphoreType.DMA((10, 10)),
-            pltpu.SemaphoreType.DMA((10, 10)),
+            pltpu.SemaphoreType.DMA((SENT, 10)),
+            pltpu.SemaphoreType.DMA((SENT, 10)),
             pltpu.SemaphoreType.DMA((3, 2)),
             pltpu.SemaphoreType.DMA((3, 2)),
         ]

time: 83.4 us -> 68.9 us (0.83)
  Pallas kernels: 79.8 us -> 65.7 us
    pallas_call x1, Pallas kernels: 79.8 us -> 65.7 us  [body(): pl.pallas_call(functools.partial(kernel, both, sizes), out_shape=[jax.Sha...]
where the time goes in v3:
time: 68.9 us; the launch traced here: 68.7 us
  Pallas kernels  65.7 us (95%)
  local copies, waits for them, and re-layouts  2.36 us (3%)
    pallas_call x1, Pallas kernels, body(): pl.pallas_call(functools.partial(kernel, both, sizes), out_shape=[jax.Sha...  65.7 us
    unnamed x4, local copies, waits for them, and re-layouts  2.36 us

profile of v3, /device:TPU:1, one launch (start us, length us, event | category | flops | bytes accessed | tf_op | source)
XLA Modules:
  0.0 68.7 jit_solution(2150980895344664577)
XLA Ops:
  0.6 65.7 %shard_map.167 = (f32[32,8,256]{2,1,0:T(8,128)}, f32[64,4,128]{2,1,0:T(4,128)}) custom-call(bf16[32,8,256]{2,1,0:T(8,128)(2,1)} %refs_0_.1, bf16[64,4,128]{2,1,0:T(4,128)(2,1)} %refs_1_.1, bf16[32,8,256]{2,1,0:T(8,128)(2,1)} %refs_2_.1, bf16[64,4,128]{2,1,0:T(4,128)(2,1)} %refs_3_.1, f32[32,8,256]{2,1,0:T(8,128)} %refs_4_.1, f32[64,4,128]{2,1,0:T(4,128)} %refs_5_.1, ...), custom_call_target="tpu_custom_call" | custom-call | tf_op jit(solution)/shard_map/pallas_call | solution.py:666
  66.4 0.0 copy-start
  66.4 1.7 %copy.20 = f32[32,8,256]{2,1,0:T(8,128)} copy(f32[32,8,256]{2,1,0:T(8,128)} %get-tuple-element.4) | data formatting | bytes 524288
  68.1 0.0 copy-done
  68.1 0.7 copy.21
Async XLA Ops:
  66.4 1.7 %copy-start = (f32[64,4,128]{2,1,0:T(4,128)S(1)}, f32[64,4,128]{2,1,0:T(4,128)}, u32[]{:S(2)}) copy-start(f32[64,4,128]{2,1,0:T(4,128)} %get-tuple-element.5) | copy-start | bytes 393220

commit v4 on v3

--- a/solution.py
+++ b/solution.py
@@ -121,24 +121,25 @@
 
 def narrow(s, weights, h, z):
     n, W = s.n, s.W
-
     for b in range(0, s.cells, 256):
         total = dot(weights[0], h[:, b : b + 256])
         for i in (1, 2):
             total = total + dot(weights[i], h[:, b + i * W : b + i * W + 256])
-        z[:, b : b + 256] = total
+        z[0 : total.shape[0], b : b + 256] = total
     edges = [dot(weights[i], h[:, s.main :]) for i in range(3)]
     total = edges[0] + roll(edges[1], -8) + roll(edges[2], -16)
     q = lanes_of((n, 128)) % 8
-    joined = jnp.where(q == 1, roll(total[:n], 1), roll(total[2 * n :], -3))
+    joined = []
+    for g in range(0, total.shape[0], 3 * n):
+        joined.append(jnp.where(q == 1, roll(total[g : g + n], 1), roll(total[g + 2 * n : g + 3 * n], -3)))
     lane = lanes_of((n, W))
 
-    def row(r):
-        at = slice(r * W, (r + 1) * W)
-        t = wide_lanes(roll(joined, -(8 * r + 1)), W)
-        left = jnp.where(lane == 0, t, roll(z[0:n, at], 1))
-        right = jnp.where(lane == W - 1, t, roll(z[2 * n : 3 * n, at], -1))
-        return left + z[n : 2 * n, at] + right
+    def row(r, g=0):
+        at, base = slice(r * W, (r + 1) * W), 3 * n * g
+        t = wide_lanes(roll(joined[g], -(8 * r + 1)), W)
+        left = jnp.where(lane == 0, t, roll(z[base : base + n, at], 1))
+        right = jnp.where(lane == W - 1, t, roll(z[base + 2 * n : base + 3 * n, at], -1))
+        return left + z[base + n : base + 2 * n, at] + right
 
     return row
 
@@ -154,13 +155,15 @@
     ) = refs
     (xm_f, xm_c, x3_f, x3_c, x9_f, x9_c,
      nm_f, nm_c, ls_f, ls_c, hg_f, hg_c, hb_f, hb_c, kc_f, kc_c, kp_f, kp_c,
-     z_f, z_c, sl_f, sl_c, e_f, e_c, mk_f, mk_c, ga_f, ga_c, sh_f, sh_c,
-     a1_f, a1_c, a3_f, a3_c, a4_f, a4_c, dup, split, rt, rw, u4, stack_f, stack_c, taps,
+     z_f, z_c, sl_f, sl_c, e_f, e_c, zn_f, zn_c, mk_f, mk_c, ga_f, ga_c, sh_f, sh_c,
+     a1_f, a1_c, a3_f, a3_c, a4_f, a4_c, ag_f, ag_c, zg_f, zg_c, one_f, one_c, two_f, two_c, dup, split, rt, rw, u4, stack_f, stack_c, taps,
      pk, pr, corner, corners, ar_a, ar_b, halo_send, halo_recv, ar_send, ar_recv) = rest
     xm, x3, x9 = (xm_f, xm_c), (x3_f, x3_c), (x9_f, x9_c)
     nm, ls, hg, hb = (nm_f, nm_c), (ls_f, ls_c), (hg_f, hg_c), (hb_f, hb_c)
     kc, kp, zs, sl, es, mk = (kc_f, kc_c), (kp_f, kp_c), (z_f, z_c), (sl_f, sl_c), (e_f, e_c), (mk_f, mk_c)
     ga, sh, a1, a3, a4 = (ga_f, ga_c), (sh_f, sh_c), (a1_f, a1_c), (a3_f, a3_c), (a4_f, a4_c)
+    zn = (zn_f, zn_c)
+    ag, zg, one, two = (ag_f, ag_c), (zg_f, zg_c), (one_f, one_c), (two_f, two_c)
     first, second = (fine_first, coarse_first), (fine_second, coarse_second)
     cot, state = (fine_cot, coarse_cot), (fine_state, coarse_state)
     inject, outs = (fine_inject, coarse_inject), (fine_out, coarse_out)
@@ -339,6 +342,11 @@
             back = slice((8 - t) * n, (9 - t) * n)
             a4[s][(8 - t) // 3, (8 - t) % 3 * n : ((8 - t) % 3 + 1) * n, :] = first[s][t * n : (t + 1) * n, :]
             taps[back, 0:w] = second[s][t // 3, (t % 3) * n : (t % 3 + 1) * n, :]
+        group = lanes_of((1, w)) // streams[s].gs
+        for g in range(GROUPS):
+            chosen = jnp.where(group == g, 1.0, 0.0).astype(BF16)
+            for i in range(3):
+                ag[s][i, 3 * n * g : 3 * n * (g + 1), :] = a4[s][i] * chosen
         a1[s][...] = first[s][...].T
         a3[s][...] = taps[0 : 9 * n, 0:w].T
         same = subs_of((w, w)) == lanes_of((w, w))
@@ -409,7 +417,18 @@
         sums.append(group_loop(s, *own_chunks(s), 2, squares))
     reduce_start(0, to_row(flat(sums, 0) + flat(sums, 1)))
     spread_wide(COT, a1, kc, ring=False)
+
+    def group_images(fields):
+        for s in both:
+            got = narrow(streams[s], ag[s], hb[s], zg[s])
+            for g in range(GROUPS):
+                for r in range(streams[s].R):
+                    fields[s][g, :, r * streams[s].W : (r + 1) * streams[s].W] = got(r, g)
+
     reduce_middle(0)
+    for s in both:
+        hb[s][...] = jnp.broadcast_to(mk[s][...], hb[s].shape).astype(BF16)
+    group_images(one)
     stats = reduce_end(0)
 
     lane = lanes_of((1, 128))
@@ -418,6 +437,7 @@
     mean_row = stats * per
     variance = roll(mean_row, -8) - mean_row * mean_row
     inverse_row = jnp.where(lane < 8, lax.rsqrt(variance + EPSILON), 0.0)
+    weight = (inverse_row + roll(inverse_row, 8)) * per
     means = [[pick(mean_row, s * GROUPS + g) for g in range(GROUPS)] for s in both]
     inverses = [[pick(inverse_row, s * GROUPS + g) for g in range(GROUPS)] for s in both]
 
@@ -500,8 +520,15 @@
         sums.append(group_loop(s, *ring_chunks(s), 2, pushed))
     reduce_start(1, to_row(flat(sums, 0) + flat(sums, 1)))
 
+    for s in both:
+        for g in range(GROUPS):
+            at = slice(g * streams[s].gs, (g + 1) * streams[s].gs)
+            for k in range(streams[s].NL // 128):
+                hb[s][at, block(k, 128)] = masked(s, k, nm[s][at, block(k, 128)]).astype(BF16)
+    group_images(two)
+
+    reduce_middle(1)
     spread_wide(TOTAL0, a3, hg)
-    reduce_middle(1)
     along = []
     for s in both:
 
@@ -510,31 +537,38 @@
             return x, x * nm[s][at, block(k, 128)]
 
         along.append(group_loop(s, *ring_chunks(s), 2, cot_sums))
-    found = reduce_end(1)
-
-    def image(row_sums):
-        scaled_mean = row_sums * per
-        got = []
+
+    def uncentred():
         for s in both:
             gs = streams[s].gs
             for g in range(GROUPS):
                 at = slice(g * gs, (g + 1) * gs)
-                one, two = pick(scaled_mean, s * GROUPS + g), pick(scaled_mean, 8 + s * GROUPS + g)
-
                 for k in range(streams[s].NL // 128):
                     here = block(k, 128)
-                    scaled = hg[s][at, here] * ls[s][at, here]
-                    grad = inverses[s][g] * (scaled - one - nm[s][at, here] * two)
-                    hb[s][at, here] = (grad * mk[s][:, here]).astype(BF16)
-            got.append(narrow(streams[s], a4[s], hb[s], zs[s]))
-        return got
-
-    got = image(found)
-    for s in both:
-        made = [got[s](r) for r in range(streams[s].R)]
+                    hb[s][at, here] = (inverses[s][g] * (hg[s][at, here] * ls[s][at, here])).astype(BF16)
+            got = narrow(streams[s], a4[s], hb[s], zs[s])
+            for r in range(streams[s].R):
+                zn[s][:, r * streams[s].W : (r + 1) * streams[s].W] = got(r)
+
+    def centred(row_sums):
+        scaled_mean = row_sums * weight
+        picked = [[[pick(scaled_mean, 8 * t + s * GROUPS + g) for g in range(GROUPS)] for t in range(2)] for s in both]
+
+        def rows_of(s, r):
+            at = slice(r * streams[s].W, (r + 1) * streams[s].W)
+            value = zn[s][:, at]
+            for g in range(GROUPS):
+                value = value - picked[s][0][g] * one[s][g, :, at] - picked[s][1][g] * two[s][g, :, at]
+            return value
+
+        return rows_of
+
+    uncentred()
+    rows_of = centred(reduce_end(1))
+    for s in both:
         for r in range(streams[s].R):
-            es[s][:, r * streams[s].W : (r + 1) * streams[s].W] = made[r]
-        put_rows(streams[s], made, xm[s].at[IMAGE])
+            es[s][:, r * streams[s].W : (r + 1) * streams[s].W] = rows_of(s, r)
+        put_rows(streams[s], [own_row(s, es[s], r) for r in range(streams[s].R)], xm[s].at[IMAGE])
     total(lambda s, r: own_row(s, es[s], r), TOTAL1)
 
     gram = [jnp.zeros((8, 128), F32) for _ in range(3)]
@@ -577,10 +611,10 @@
                 crossed[t] = crossed[t] + pairs[s][t][g] * inverses[s][g]
     entries = flat(sums, 0) + flat(sums, 1) + flat(along, 0) + flat(along, 1) + flat(image_sums, 0) + flat(image_sums, 1)
     reduce_start(2, to_row(entries + gram + crossed))
+    uncentred()
     reduce_middle(2)
     found = reduce_end(2)
 
-    weight = (inverse_row + roll(inverse_row, 8)) * per
     cc, c0, g00, cq, pq = [pick(found, 48 + k) for k in range(5)]
     c1 = cq - jnp.sum(found * weight * roll(found, -16), axis=1, keepdims=True)
     g01 = pq - jnp.sum(found * weight * roll(found, -32), axis=1, keepdims=True)
@@ -594,10 +628,10 @@
     by0 = 1.0 - m0 / d0 + (m1 / d1) * (turn / d0)
     by1 = alpha * (1.0 - m1 / d1)
 
-    got = image(found)
+    rows_of = centred(found)
     for s in both:
         for r in range(streams[s].R):
-            outs[s][:, r, :] = cot[s][:, r, :] + by0 * own_row(s, es[s], r) + by1 * got[s](r)
+            outs[s][:, r, :] = cot[s][:, r, :] + by0 * own_row(s, es[s], r) + by1 * rows_of(s, r)
 
     for k in range(SENT):
         exchange_end(k)
@@ -635,12 +669,17 @@
             (lambda s: (3 * s.n, s.cells), F32),
             (lambda s: (s.n, s.cells), F32),
             (lambda s: (s.n, s.cells), F32),
+            (lambda s: (s.n, s.cells), F32),
             (lambda s: (1, s.NL), F32),
             (lambda s: (s.w, 128), F32),
             (lambda s: (s.w, 128), F32),
             (lambda s: (s.w, 9 * s.n), BF16),
             (lambda s: (s.w, 9 * s.n), BF16),
             (lambda s: (3, 3 * s.n, s.w), BF16),
+            (lambda s: (3, GROUPS * 3 * s.n, s.w), BF16),
+            (lambda s: (GROUPS * 3 * s.n, s.cells), F32),
+            (lambda s: (GROUPS, s.n, s.cells), F32),
+            (lambda s: (GROUPS, s.n, s.cells), F32),
         ):
             scratch += [vmem(shape(s), dtype) for s in both]
         scratch += [
@@ -673,7 +712,6 @@
                 collective_id=0, has_side_effects=True, vmem_limit_bytes=56 * 1024 * 1024
             ),
         )(*args)
-
     field = P(None, "row", "col")
     return jax.shard_map(
         body,

time: 68.9 us -> 66.1 us (0.959)
  Pallas kernels: 65.7 us -> 62.9 us
    pallas_call x1, Pallas kernels: 65.7 us -> 62.9 us  [body(): pl.pallas_call(functools.partial(kernel, both, sizes), out_shape=[jax.Sha...]
where the time goes in v4:
time: 66.1 us; the launch traced here: 65.9 us
  Pallas kernels  62.9 us (95%)
  local copies, waits for them, and re-layouts  2.36 us (4%)
    pallas_call x1, Pallas kernels, body(): pl.pallas_call(functools.partial(kernel, both, sizes), out_shape=[jax.Sha...  62.9 us
    unnamed x4, local copies, waits for them, and re-layouts  2.36 us

profile of v4, /device:TPU:1, one launch (start us, length us, event | category | flops | bytes accessed | tf_op | source)
XLA Modules:
  0.0 65.9 jit_solution(15085694909138839455)
XLA Ops:
  0.6 62.9 %shard_map.167 = (f32[32,8,256]{2,1,0:T(8,128)}, f32[64,4,128]{2,1,0:T(4,128)}) custom-call(bf16[32,8,256]{2,1,0:T(8,128)(2,1)} %refs_0_.1, bf16[64,4,128]{2,1,0:T(4,128)(2,1)} %refs_1_.1, bf16[32,8,256]{2,1,0:T(8,128)(2,1)} %refs_2_.1, bf16[64,4,128]{2,1,0:T(4,128)(2,1)} %refs_3_.1, f32[32,8,256]{2,1,0:T(8,128)} %refs_4_.1, f32[64,4,128]{2,1,0:T(4,128)} %refs_5_.1, ...), custom_call_target="tpu_custom_call" | custom-call | tf_op jit(solution)/shard_map/pallas_call | solution.py:705
  63.6 0.0 copy-start
  63.6 1.7 %copy.20 = f32[32,8,256]{2,1,0:T(8,128)} copy(f32[32,8,256]{2,1,0:T(8,128)} %get-tuple-element.4) | data formatting | bytes 524288
  65.3 0.0 copy-done
  65.3 0.7 copy.21
Async XLA Ops:
  63.6 1.7 %copy-start = (f32[64,4,128]{2,1,0:T(4,128)S(1)}, f32[64,4,128]{2,1,0:T(4,128)}, u32[]{:S(2)}) copy-start(f32[64,4,128]{2,1,0:T(4,128)} %get-tuple-element.5) | copy-start | bytes 393220

commit v5 on v4

--- a/solution.py
+++ b/solution.py
@@ -146,13 +146,17 @@
 
 def kernel(streams, sizes, *refs):
     f, c = streams
+    far, refs = refs[:10], refs[10:]
     (
-        fine_state, coarse_state, fine_inject, coarse_inject, fine_cot, coarse_cot,
-        fine_first, fine_second, coarse_first, coarse_second,
         fine_gain, fine_shift, coarse_gain, coarse_shift, reduction, up,
         fine_out, coarse_out,
         *rest,
     ) = refs
+    near, load_sem, rest = rest[:10], rest[10], rest[11:]
+    (
+        fine_state, coarse_state, fine_inject, coarse_inject, fine_cot, coarse_cot,
+        fine_first, fine_second, coarse_first, coarse_second,
+    ) = near
     (xm_f, xm_c, x3_f, x3_c, x9_f, x9_c,
      nm_f, nm_c, ls_f, ls_c, hg_f, hg_c, hb_f, hb_c, kc_f, kc_c, kp_f, kp_c,
      z_f, z_c, sl_f, sl_c, e_f, e_c, zn_f, zn_c, mk_f, mk_c, ga_f, ga_c, sh_f, sh_c,
@@ -302,6 +306,9 @@
             ref = buf.at[k, pl.ds(0, size - 1)]
             pltpu.make_async_copy(ref, ref, ar_send.at[k, stage]).wait()
 
+    loads = [pltpu.make_async_copy(a, b, load_sem.at[k]) for k, (a, b) in enumerate(zip(far, near))]
+    for copy in loads:
+        copy.start()
     for s in both:
         W, R = streams[s].W, streams[s].R
         for k in range(SENT):
@@ -327,11 +334,15 @@
 
     lax.fori_loop(1, size_a, greet_a, 0)
     lax.fori_loop(1, size_b, greet_b, 0)
+    for copy in loads[:2]:
+        copy.wait()
     for s in both:
         put_rows(streams[s], [state[s][:, r, :] for r in range(streams[s].R)], xm[s].at[STATE])
     beside = sum(has(d).astype(jnp.int32) for d in DIRS)
     pl.semaphore_wait(barrier, beside + (size_a + size_b - 2))
     exchange_start(STATE)
+    for copy in loads[2:]:
+        copy.wait()
     for s in both:
         put_rows(streams[s], [cot[s][:, r, :] for r in range(streams[s].R)], xm[s].at[COT])
     pack_own(COT)
@@ -655,7 +666,7 @@
             args[k + 1] = args[k + 1].reshape(3, 3 * s.n, s.w)
         args[14] = args[14].transpose(0, 1, 3, 2).reshape(4 * f.n, c.n)
         vmem = pltpu.VMEM
-        scratch = []
+        scratch = [vmem(a.shape, a.dtype) for a in args[:10]] + [pltpu.SemaphoreType.DMA((10,))]
         for shape, dtype in (
             (lambda s: (5, s.n, (s.R + 4) * s.W), BF16),
             (lambda s: (3 * s.n, (s.R + 4) * s.W), BF16),
@@ -705,7 +716,7 @@
         return pl.pallas_call(
             functools.partial(kernel, both, sizes),
             out_shape=[jax.ShapeDtypeStruct(a.shape, F32) for a in args[4:6]],
-            in_specs=[pl.BlockSpec(memory_space=pltpu.VMEM)] * 16,
+            in_specs=[pl.BlockSpec(memory_space=pl.ANY)] * 10 + [pl.BlockSpec(memory_space=pltpu.VMEM)] * 6,
             out_specs=[pl.BlockSpec(memory_space=pltpu.VMEM)] * 2,
             scratch_shapes=scratch,
             compiler_params=pltpu.CompilerParams(

time: 66.1 us -> 65.5 us (level)
  no operation moved by 1% of the time
where the time goes in v5:
time: 65.5 us; the launch traced here: 65.3 us
  Pallas kernels  62.3 us (95%)
  local copies, waits for them, and re-layouts  2.36 us (4%)
    pallas_call x1, Pallas kernels, body(): pl.pallas_call(functools.partial(kernel, both, sizes), out_shape=[jax.Sha...  62.3 us
    unnamed x4, local copies, waits for them, and re-layouts  2.36 us

profile of v5, /device:TPU:1, one launch (start us, length us, event | category | flops | bytes accessed | tf_op | source)
XLA Modules:
  0.0 65.3 jit_solution(13095029368466640386)
XLA Ops:
  0.6 62.3 %shard_map.167 = (f32[32,8,256]{2,1,0:T(8,128)}, f32[64,4,128]{2,1,0:T(4,128)}) custom-call(bf16[32,8,256]{2,1,0:T(8,128)(2,1)} %refs_0_.1, bf16[64,4,128]{2,1,0:T(4,128)(2,1)} %refs_1_.1, bf16[32,8,256]{2,1,0:T(8,128)(2,1)} %refs_2_.1, bf16[64,4,128]{2,1,0:T(4,128)(2,1)} %refs_3_.1, f32[32,8,256]{2,1,0:T(8,128)} %refs_4_.1, f32[64,4,128]{2,1,0:T(4,128)} %refs_5_.1, ...), custom_call_target="tpu_custom_call" | custom-call | tf_op jit(solution)/shard_map/pallas_call | solution.py:716
  62.9 0.0 copy-start
  62.9 1.7 %copy.20 = f32[32,8,256]{2,1,0:T(8,128)} copy(f32[32,8,256]{2,1,0:T(8,128)} %get-tuple-element.4) | data formatting | bytes 524288
  64.6 0.0 copy-done
  64.6 0.7 %copy.21 = f32[64,4,128]{2,1,0:T(4,128)} copy(f32[64,4,128]{2,1,0:T(4,128)S(1)} %copy-done) | data formatting | bytes 262144
Async XLA Ops:
  62.9 1.7 %copy-start = (f32[64,4,128]{2,1,0:T(4,128)S(1)}, f32[64,4,128]{2,1,0:T(4,128)}, u32[]{:S(2)}) copy-start(f32[64,4,128]{2,1,0:T(4,128)} %get-tuple-element.5) | copy-start | bytes 393220

commit v6 on v5

--- a/solution.py
+++ b/solution.py
@@ -180,17 +180,27 @@
     def has(d):
         return (row + d[0] >= 0) & (row + d[0] < rows) & (col + d[1] >= 0) & (col + d[1] < cols)
 
-    size_a, size_b = low_rows * high_cols, high_rows * low_cols
-    me_a = (row % low_rows) * high_cols + col // low_cols
-    me_b = (row // low_rows) * low_cols + col % low_cols
-
-    def peer_a(k):
-        p = (me_a + k) % size_a
-        return ((row // low_rows) * low_rows + p // high_cols, (p % high_cols) * low_cols + col % low_cols)
-
-    def peer_b(k):
-        p = (me_b + k) % size_b
-        return ((p // low_cols) * low_rows + row % low_rows, (col // low_cols) * low_cols + p % low_cols)
+    nx, ny = low_rows // 2, high_cols
+    nz = high_rows * low_cols
+    x, core, y = row % low_rows // 2, row % 2, col // low_cols
+    z = row // low_rows * low_cols + col % low_cols
+
+    def steps(n, at):
+        return [(at + d) % n for d in range(n)]
+
+    x_rows = [2 * v + core for v in steps(nx, x)]
+    y_cols = [v * low_cols for v in steps(ny, y)]
+    z_both = [(v // low_cols * low_rows, v % low_cols) for v in steps(nz, z)]
+
+    def hops(d):
+        return sum(min(v, n - v) for v, n in zip(d, (nx, ny, nz)))
+
+    offsets = [(a, b, c) for a in range(nx) for b in range(ny) for c in range(nz) if a or b or c]
+    offsets.sort(key=lambda d: (-hops(d), d))
+    chips = [(z_both[d][0] + x_rows[a], y_cols[b] + z_both[d][1]) for a, b, d in offsets]
+    partner = [(row + 1 - 2 * core, col)]
+    size_a, size_b = 2, nx * ny * nz
+    me_a, me_b = core, (x * ny + y) * nz + z
 
     def strips(k):
         made = []
@@ -275,15 +285,12 @@
             made.append(jnp.where(inside, sides[own_part[s]], outside))
         return made
 
-    def spread(k, stage, buf, me, size, peer):
-        def send(p, _):
+    def spread(k, stage, buf, me, peers):
+        for peer in peers:
             pltpu.make_async_remote_copy(
                 src_ref=buf.at[k, me], dst_ref=buf.at[k, me],
                 send_sem=ar_send.at[k, stage], recv_sem=ar_recv.at[k, stage],
-                device_id=peer(p), device_id_type=MESH).start()
-            return 0
-
-        lax.fori_loop(1, size, send, 0)
+                device_id=peer, device_id_type=MESH).start()
 
     def collect(k, stage, buf, size):
         ref = buf.at[k, pl.ds(0, size - 1)]
@@ -292,11 +299,11 @@
 
     def reduce_start(k, value):
         ar_a[k, me_a] = value
-        spread(k, 0, ar_a, me_a, size_a, peer_a)
+        spread(k, 0, ar_a, me_a, partner)
 
     def reduce_middle(k):
         ar_b[k, me_b] = collect(k, 0, ar_a, size_a)
-        spread(k, 1, ar_b, me_b, size_b, peer_b)
+        spread(k, 1, ar_b, me_b, chips)
 
     def reduce_end(k):
         return collect(k, 1, ar_b, size_b)
@@ -324,16 +331,8 @@
     for d in DIRS:
         pl.when(has(d))(functools.partial(greet, (row + d[0], col + d[1])))
 
-    def greet_a(k, _):
-        greet(peer_a(k))
-        return 0
-
-    def greet_b(k, _):
-        greet(peer_b(k))
-        return 0
-
-    lax.fori_loop(1, size_a, greet_a, 0)
-    lax.fori_loop(1, size_b, greet_b, 0)
+    for device in chips + partner:
+        greet(device)
     for copy in loads[:2]:
         copy.wait()
     for s in both:
@@ -427,6 +426,7 @@
 
         sums.append(group_loop(s, *own_chunks(s), 2, squares))
     reduce_start(0, to_row(flat(sums, 0) + flat(sums, 1)))
+    reduce_middle(0)
     spread_wide(COT, a1, kc, ring=False)
 
     def group_images(fields):
@@ -436,7 +436,6 @@
                 for r in range(streams[s].R):
                     fields[s][g, :, r * streams[s].W : (r + 1) * streams[s].W] = got(r, g)
 
-    reduce_middle(0)
     for s in both:
         hb[s][...] = jnp.broadcast_to(mk[s][...], hb[s].shape).astype(BF16)
     group_images(one)
@@ -531,6 +530,7 @@
         sums.append(group_loop(s, *ring_chunks(s), 2, pushed))
     reduce_start(1, to_row(flat(sums, 0) + flat(sums, 1)))
 
+    reduce_middle(1)
     for s in both:
         for g in range(GROUPS):
             at = slice(g * streams[s].gs, (g + 1) * streams[s].gs)
@@ -538,7 +538,6 @@
                 hb[s][at, block(k, 128)] = masked(s, k, nm[s][at, block(k, 128)]).astype(BF16)
     group_images(two)
 
-    reduce_middle(1)
     spread_wide(TOTAL0, a3, hg)
     along = []
     for s in both:
@@ -622,8 +621,8 @@
                 crossed[t] = crossed[t] + pairs[s][t][g] * inverses[s][g]
     entries = flat(sums, 0) + flat(sums, 1) + flat(along, 0) + flat(along, 1) + flat(image_sums, 0) + flat(image_sums, 1)
     reduce_start(2, to_row(entries + gram + crossed))
+    reduce_middle(2)
     uncentred()
-    reduce_middle(2)
     found = reduce_end(2)
 
     cc, c0, g00, cq, pq = [pick(found, 48 + k) for k in range(5)]
@@ -706,8 +705,8 @@
             vmem((SENT, 2, f.n + c.n, 128), BF16),
             vmem((SENT, 2, 16, 128), BF16),
             vmem((SENT, 4, 16, 128), BF16),
-            vmem((3, sizes[2] * (cols // sizes[3]), 1, 128), F32),
-            vmem((3, (rows // sizes[2]) * sizes[3], 1, 128), F32),
+            vmem((3, 2, 1, 128), F32),
+            vmem((3, rows * cols // 2, 1, 128), F32),
             pltpu.SemaphoreType.DMA((SENT, 10)),
             pltpu.SemaphoreType.DMA((SENT, 10)),
             pltpu.SemaphoreType.DMA((3, 2)),

time: 65.5 us -> 64.4 us (0.983)
  Pallas kernels: 62.3 us -> 61.3 us
    pallas_call x1, Pallas kernels: 62.3 us -> 61.3 us  [body(): pl.pallas_call(functools.partial(kernel, both, sizes), out_shape=[jax.Sha...]
where the time goes in v6:
time: 64.4 us; the launch traced here: 64.3 us
  Pallas kernels  61.3 us (95%)
  local copies, waits for them, and re-layouts  2.36 us (4%)
  between operations  0.65 us (1%)
    pallas_call x1, Pallas kernels, body(): pl.pallas_call(functools.partial(kernel, both, sizes), out_shape=[jax.Sha...  61.3 us
    unnamed x4, local copies, waits for them, and re-layouts  2.36 us

profile of v6, /device:TPU:1, one launch (start us, length us, event | category | flops | bytes accessed | tf_op | source)
XLA Modules:
  0.0 64.3 jit_solution(3451014838824998610)
XLA Ops:
  0.6 61.3 %shard_map.167 = (f32[32,8,256]{2,1,0:T(8,128)}, f32[64,4,128]{2,1,0:T(4,128)}) custom-call(bf16[32,8,256]{2,1,0:T(8,128)(2,1)} %refs_0_.1, bf16[64,4,128]{2,1,0:T(4,128)(2,1)} %refs_1_.1, bf16[32,8,256]{2,1,0:T(8,128)(2,1)} %refs_2_.1, bf16[64,4,128]{2,1,0:T(4,128)(2,1)} %refs_3_.1, f32[32,8,256]{2,1,0:T(8,128)} %refs_4_.1, f32[64,4,128]{2,1,0:T(4,128)} %refs_5_.1, ...), custom_call_target="tpu_custom_call" | custom-call | tf_op jit(solution)/shard_map/pallas_call | solution.py:715
  61.9 0.0 copy-start
  61.9 1.7 %copy.20 = f32[32,8,256]{2,1,0:T(8,128)} copy(f32[32,8,256]{2,1,0:T(8,128)} %get-tuple-element.4) | data formatting | bytes 524288
  63.6 0.0 copy-done
  63.6 0.7 %copy.21 = f32[64,4,128]{2,1,0:T(4,128)} copy(f32[64,4,128]{2,1,0:T(4,128)S(1)} %copy-done) | data formatting | bytes 262144
Async XLA Ops:
  61.9 1.7 %copy-start = (f32[64,4,128]{2,1,0:T(4,128)S(1)}, f32[64,4,128]{2,1,0:T(4,128)}, u32[]{:S(2)}) copy-start(f32[64,4,128]{2,1,0:T(4,128)} %get-tuple-element.5) | copy-start | bytes 393220
